TPU v7x, 512 devices: a whole 4x4x16 slice. The times are simulated.
512 devices in a mesh: bx: 32 (over x_hi, z), by: 16 (over x_lo, y, core).
Axes of the slice: x: 4 (x_hi: 2, x_lo: 2; x = x_hi * 2 + x_lo), y: 4, z: 16, core: 2. Of those that a mesh axis runs over, the one named last changes fastest.
Arguments:
- charges: float32 [32, 16, 2048, 128], P('bx', 'by'), may hold values from -6 to 6
- speed: float32 [32, 16, 2048], P('bx', 'by'), may hold values from 0.5 to 2
- omega: float32 [4, 64], replicated, may hold values from -3.140625 to 3.140625
- mixers: float32 [4, 2, 2, 128, 128], replicated, may hold values from -0.375 to 0.375
- source_map: float32 [128, 128], replicated, may hold values from -0.5 to 0.5
- target_map: float32 [128, 1024], replicated, may hold values from -0.5 to 0.5
Outputs:
- targets: bfloat16 [32, 16, 2048, 1024], P('bx', 'by')
All inputs are finite; a program needn't handle non-finite values.
Results may differ from a plain program's by a relative error of at most 0.001.
Values sent between devices are 32-bit elements; how exact they have to be, the bound alone decides.
A program may use at most 64 MiB of HBM per device.

v0:
```python
import jax
import jax.numpy as jnp
from jax import lax
from jax.sharding import PartitionSpec as P

LEVELS = 4


HIGH = lax.Precision.HIGHEST


def partner(value, axis, distance):
    mask = 2**distance
    pairs = [(source, source ^ mask) for source in range(lax.axis_size(axis))]
    return lax.ppermute(value, axis, pairs)


def rotate(weights, angles):
    half = weights.shape[-1] // 2
    real_part = weights[..., :half]
    imag_part = weights[..., half:]
    cosine = jnp.cos(angles)
    sine = jnp.sin(angles)
    return jnp.concatenate(
        [real_part * cosine - imag_part * sine, real_part * sine + imag_part * cosine], axis=-1
    )


def pick_matrix(level_mix, target_half, child):
    row = lax.dynamic_index_in_dim(level_mix, target_half, 0, False)
    return lax.dynamic_index_in_dim(row, child, 0, False)


def partner_weights(rotated, on_first, bit):
    if on_first:
        return partner(rotated, "bx", bit)
    return partner(rotated, "by", bit)


def level_bit(parity, axis_count):
    if parity == 0:
        return 0
    return axis_count.bit_length() - 2


def shards(charges, speed, omega, mixers, source_map, target_map):
    box_count = charges.shape[2]
    flat_charges = charges.reshape(box_count, charges.shape[3])
    box_speed = speed.reshape(box_count, 1)
    weights = jnp.matmul(flat_charges, source_map, precision=HIGH)
    half_levels = LEVELS // 2
    first_count = lax.axis_size("bx")
    second_count = lax.axis_size("by")
    for level in range(LEVELS):
        on_first = level < half_levels
        if on_first:
            position = lax.axis_index("bx")
            bit = level_bit(level % half_levels, first_count)
        else:
            position = lax.axis_index("by")
            bit = level_bit(level % half_levels, second_count)
        side = position // 2**bit % 2
        rotated = rotate(weights, box_speed * omega[level][None, :])
        level_mix = mixers[level]
        own_matrix = pick_matrix(level_mix, side, side)
        other_matrix = pick_matrix(level_mix, side, 1 - side)
        received = partner_weights(rotated, on_first, bit)
        weights = jnp.matmul(rotated, own_matrix, precision=HIGH) + jnp.matmul(
            received, other_matrix, precision=HIGH
        )
    result = jnp.matmul(weights, target_map, precision=HIGH).astype(jnp.bfloat16)
    return result.reshape(1, 1, box_count, target_map.shape[1])


def solution(mesh):
    placed = (P("bx", "by", None, None), P("bx", "by", None), P(), P(), P(), P())
    return jax.shard_map(
        shards, mesh=mesh, in_specs=placed, out_specs=P("bx", "by", None, None), check_vma=False
    )
```

profile of v0, /device:TPU:1, one launch (start us, length us, event | category | flops | bytes accessed | tf_op | source)
XLA Modules:
  0.0 120.2 jit_solution(14163375988348203059)
XLA Ops:
  0.0 0.0 copy-start
  0.0 0.9 slice_bitcast_fusion
  0.9 0.4 copy-done
  1.3 1.9 %fusion = f32[2048,128]{0,1:T(8,128)S(1)} fusion(f32[128,128]{1,0:T(8,128)} %param.10, f32[1,1,2048,128]{3,2,1,0:T(8,128)S(1)} %copy-done), kind=kOutput, calls=%fused_computation.9 | convolution fusion | flops 402653184 | bytes 2162688 | tf_op jit(solution)/shard_map/dot_general | solution.py:50
  3.2 2.8 %fusion.24 = (f32[2048,64]{0,1:T(8,128)S(1)}, f32[2048,64]{0,1:T(8,128)S(1)}) fusion(f32[2048,128]{0,1:T(8,128)S(1)} %fusion, f32[64]{0:T(128)S(1)} %get-tuple-element.19, f32[2048]{0:T(1024)} %bitcast.45), kind=kLoop, calls=%fused_computation.41 | loop fusion | flops 917504 | bytes 2105600 | tf_op jit(solution)/shard_map/sub | solution.py:25
  6.0 1.0 pad_maximum_fusion
  7.1 4.5 %collective-permute-start = (f32[2048,128]{0,1:T(8,128)}, f32[2048,128]{0,1:T(8,128)}, u32[]{:S(2)}, u32[]{:S(2)}) collective-permute-start(f32[2048,128]{0,1:T(8,128)} %pad_maximum_fusion), channel_id=1, source_target_pairs={{0,16},{16,0},{32,48},{48,32},{64,80},{80,64},{96,112},{112,96},{1... | collective-permute-start | bytes 3145736 | tf_op jit(solution)/shard_map/ppermute | solution.py:15
  11.6 0.0 copy-done.1
  11.6 0.9 fusion.54
  12.5 1.1 fusion.36
  13.6 16.6 %collective-permute-done = f32[2048,128]{0,1:T(8,128)} collective-permute-done((f32[2048,128]{0,1:T(8,128)}, f32[2048,128]{0,1:T(8,128)}, u32[]{:S(2)}, u32[]{:S(2)}) %collective-permute-start) | collective-permute-done | bytes 1048608 | tf_op jit(solution)/shard_map/ppermute | solution.py:15
  30.2 2.3 %convolution_add_fusion.3 = f32[2048,128]{0,1:T(8,128)S(1)} fusion(f32[2048,128]{0,1:T(8,128)S(1)} %fusion.36, f32[2048,128]{0,1:T(8,128)} %collective-permute-done, f32[1,2,2,128,128]{4,3,2,1,0:T(8,128)S(1)} %get-tuple-element.13, s32[]{:T(128)S(6)} %select_n.80, s32[]{:T(128)S(6)} %select_n.82), kind=kOutput, calls=%fused_computation.4 | convolution fusion | flops 402915328 | bytes 3211272 | tf_op jit(solution)/shard_map/dot_general | solution.py:68
  32.5 2.1 %fusion.22 = (f32[2048,64]{0,1:T(8,128)S(1)}, f32[2048,64]{0,1:T(8,128)S(1)}) fusion(f32[2048,128]{0,1:T(8,128)S(1)} %convolution_add_fusion.3, f32[64]{0:T(128)S(1)} %get-tuple-element.18, f32[2048]{0:T(1024)S(1)} %bitcast.46), kind=kLoop, calls=%fused_computation.39 | loop fusion | flops 917504 | bytes 2105600 | tf_op jit(solution)/shard_map/sub | solution.py:25
  34.6 1.0 pad_maximum_fusion.1
  35.7 9.1 %collective-permute-start.1 = (f32[2048,128]{0,1:T(8,128)}, f32[2048,128]{0,1:T(8,128)S(1)}, u32[]{:S(2)}, u32[]{:S(2)}) collective-permute-start(f32[2048,128]{0,1:T(8,128)} %pad_maximum_fusion.1), channel_id=1, source_target_pairs={{0,256},{16,272},{32,288},{48,304},{64,320},{80,336},{96,352},{112... | collective-permute-start | bytes 3145736 | tf_op jit(solution)/shard_map/ppermute | solution.py:15
  44.9 1.9 %fusion.33 = f32[2048,128]{0,1:T(8,128)S(1)} fusion(f32[1,2,2,128,128]{4,3,2,1,0:T(8,128)} %get-tuple-element.14, s32[]{:T(128)S(6)} %select_n.86, f32[2048,64]{0,1:T(8,128)S(1)} %get-tuple-element.10, f32[2048,64]{0,1:T(8,128)S(1)} %get-tuple-element.9), kind=kOutput, calls=%fused_computation.50 | convolution fusion | flops 402915328 | bytes 2162692 | tf_op jit(solution)/shard_map/dot_general | solution.py:68
  46.8 19.9 %collective-permute-done.1 = f32[2048,128]{0,1:T(8,128)S(1)} collective-permute-done((f32[2048,128]{0,1:T(8,128)}, f32[2048,128]{0,1:T(8,128)S(1)}, u32[]{:S(2)}, u32[]{:S(2)}) %collective-permute-start.1) | collective-permute-done | bytes 1048608 | tf_op jit(solution)/shard_map/ppermute | solution.py:15
  66.7 1.9 %convolution_add_fusion.2 = f32[2048,128]{0,1:T(8,128)S(1)} fusion(f32[2048,128]{0,1:T(8,128)S(1)} %fusion.33, f32[2048,128]{0,1:T(8,128)S(1)} %collective-permute-done.1, f32[1,2,2,128,128]{4,3,2,1,0:T(8,128)} %get-tuple-element.14, s32[]{:T(128)S(6)} %select_n.86, s32[]{:T(128)S(6)} %select_n.88), kind=kOutput, calls=%fused_computation.3 | convolution fusion | flops 402915328 | bytes 3211272 | tf_op jit(solution)/shard_map/dot_general | solution.py:68
  68.6 2.1 %fusion.20 = (f32[2048,64]{0,1:T(8,128)S(1)}, f32[2048,64]{0,1:T(8,128)S(1)}) fusion(f32[2048,128]{0,1:T(8,128)S(1)} %convolution_add_fusion.2, f32[64]{0:T(128)S(1)} %get-tuple-element.20, f32[2048]{0:T(1024)S(1)} %bitcast.47), kind=kLoop, calls=%fused_computation.37 | loop fusion | flops 917504 | bytes 2105600 | tf_op jit(solution)/shard_map/sub | solution.py:25
  70.7 1.0 pad_maximum_fusion.2
  71.8 4.5 %collective-permute-start.2 = (f32[2048,128]{0,1:T(8,128)}, f32[2048,128]{0,1:T(8,128)S(1)}, u32[]{:S(2)}, u32[]{:S(2)}) collective-permute-start(f32[2048,128]{0,1:T(8,128)} %pad_maximum_fusion.2), channel_id=1, source_target_pairs={{0,1},{1,0},{2,3},{3,2},{4,5},{5,4},{6,7},{7,6},{8,9},{9,8},{10,11... | collective-permute-start | bytes 3145736 | tf_op jit(solution)/shard_map/ppermute | solution.py:15
  76.3 1.9 %fusion.30 = f32[2048,128]{0,1:T(8,128)S(1)} fusion(f32[1,2,2,128,128]{4,3,2,1,0:T(8,128)} %get-tuple-element.16, s32[]{:T(128)S(6)} %select_n.91, f32[2048,64]{0,1:T(8,128)S(1)} %get-tuple-element.8, f32[2048,64]{0,1:T(8,128)S(1)} %get-tuple-element.7), kind=kOutput, calls=%fused_computation.47 | convolution fusion | flops 402915328 | bytes 2162692 | tf_op jit(solution)/shard_map/dot_general | solution.py:68
  78.3 0.3 collective-permute-done.2
  78.6 1.9 %convolution_add_fusion.1 = f32[2048,128]{0,1:T(8,128)S(1)} fusion(f32[2048,128]{0,1:T(8,128)S(1)} %fusion.30, f32[2048,128]{0,1:T(8,128)S(1)} %collective-permute-done.2, f32[1,2,2,128,128]{4,3,2,1,0:T(8,128)} %get-tuple-element.16, s32[]{:T(128)S(6)} %select_n.91, s32[]{:T(128)S(6)} %select_n.93), kind=kOutput, calls=%fused_computation.2 | convolution fusion | flops 402915328 | bytes 3211272 | tf_op jit(solution)/shard_map/dot_general | solution.py:68
  80.5 2.1 %fusion.18 = (f32[2048,64]{0,1:T(8,128)S(1)}, f32[2048,64]{0,1:T(8,128)S(1)}) fusion(f32[2048,128]{0,1:T(8,128)S(1)} %convolution_add_fusion.1, f32[64]{0:T(128)S(1)} %get-tuple-element.17, f32[2048]{0:T(1024)S(1)} %bitcast.48), kind=kLoop, calls=%fused_computation.35 | loop fusion | flops 917504 | bytes 2105600 | tf_op jit(solution)/shard_map/sub | solution.py:25
  82.6 1.0 pad_maximum_fusion.3
  83.7 3.3 %collective-permute-start.3 = (f32[2048,128]{0,1:T(8,128)}, f32[2048,128]{0,1:T(8,128)S(1)}, u32[]{:S(2)}, u32[]{:S(2)}) collective-permute-start(f32[2048,128]{0,1:T(8,128)} %pad_maximum_fusion.3), channel_id=1, source_target_pairs={{0,8},{1,9},{2,10},{3,11},{4,12},{5,13},{6,14},{7,15},{8,0},{9,1},... | collective-permute-start | bytes 3145736 | tf_op jit(solution)/shard_map/ppermute | solution.py:15
  87.0 0.0 copy-start.2
  87.0 1.8 %fusion.27 = f32[2048,128]{1,0:T(8,128)S(1)} fusion(f32[1,2,2,128,128]{4,3,2,1,0:T(8,128)S(1)} %get-tuple-element.15, s32[]{:T(128)S(6)} %select_n.97, f32[2048,64]{0,1:T(8,128)S(1)} %get-tuple-element.6, f32[2048,64]{0,1:T(8,128)S(1)} %get-tuple-element.5), kind=kOutput, calls=%fused_computation.44 | convolution fusion | flops 402915328 | bytes 2162692 | tf_op jit(solution)/shard_map/dot_general | solution.py:68
  88.9 21.3 %collective-permute-done.3 = f32[2048,128]{0,1:T(8,128)S(1)} collective-permute-done((f32[2048,128]{0,1:T(8,128)}, f32[2048,128]{0,1:T(8,128)S(1)}, u32[]{:S(2)}, u32[]{:S(2)}) %collective-permute-start.3) | collective-permute-done | bytes 1048608 | tf_op jit(solution)/shard_map/ppermute | solution.py:15
  110.1 1.8 %convolution_add_fusion = f32[2048,128]{1,0:T(8,128)S(1)} fusion(f32[2048,128]{1,0:T(8,128)S(1)} %fusion.27, f32[2048,128]{0,1:T(8,128)S(1)} %collective-permute-done.3, f32[1,2,2,128,128]{4,3,2,1,0:T(8,128)S(1)} %get-tuple-element.15, s32[]{:T(128)S(6)} %select_n.97, s32[]{:T(128)S(6)} %select_n.99), kind=kOutput, calls=%fused_computation.1 | convolution fusion | flops 402915328 | bytes 3211272 | tf_op jit(solution)/shard_map/dot_general | solution.py:68
  112.0 8.2 %convert_bitcast_fusion = bf16[1,1,2048,1024]{3,2,1,0:T(8,128)(2,1)} fusion(f32[2048,128]{1,0:T(8,128)S(1)} %convolution_add_fusion, f32[128,1024]{1,0:T(8,128)S(1)} %copy-done.2), kind=kOutput, calls=%fused_computation | convolution fusion | flops 3223322624 | bytes 5767168 | tf_op jit(solution)/shard_map/dot_general | solution.py:71
  (4 shorter events, 0.0 us)
Async XLA Ops:
  0.0 1.3 %copy-start = (f32[1,1,2048,128]{3,2,1,0:T(8,128)S(1)}, f32[1,1,2048,128]{3,2,1,0:T(8,128)}, u32[]{:S(2)}) copy-start(f32[1,1,2048,128]{3,2,1,0:T(8,128)} %param.6) | copy-start | bytes 3145732
  0.0 11.6 %copy-start.1 = (f32[4,2,2,128,128]{4,3,2,1,0:T(8,128)S(1)}, f32[4,2,2,128,128]{4,3,2,1,0:T(8,128)}, u32[]{:S(2)}) copy-start(f32[4,2,2,128,128]{4,3,2,1,0:T(8,128)} %param.9) | copy-start | bytes 3145732
  7.1 25.4 %copy-start.3 = (f32[1,1,2048]{2,1,0:T(1,128)S(1)}, f32[1,1,2048]{2,1,0:T(1,128)}, u32[]{:S(2)}) copy-start(f32[1,1,2048]{2,1,0:T(1,128)} %param.7) | copy-start | bytes 24580
  7.1 23.1 %collective-permute-start = (f32[2048,128]{0,1:T(8,128)}, f32[2048,128]{0,1:T(8,128)}, u32[]{:S(2)}, u32[]{:S(2)}) collective-permute-start(f32[2048,128]{0,1:T(8,128)} %pad_maximum_fusion), channel_id=1, source_target_pairs={{0,16},{16,0},{32,48},{48,32},{64,80},{80,64},{96,112},{112,96},{1... | collective-permute-start | bytes 3145736 | tf_op jit(solution)/shard_map/ppermute | solution.py:15
  35.7 31.0 %collective-permute-start.1 = (f32[2048,128]{0,1:T(8,128)}, f32[2048,128]{0,1:T(8,128)S(1)}, u32[]{:S(2)}, u32[]{:S(2)}) collective-permute-start(f32[2048,128]{0,1:T(8,128)} %pad_maximum_fusion.1), channel_id=1, source_target_pairs={{0,256},{16,272},{32,288},{48,304},{64,320},{80,336},{96,352},{112... | collective-permute-start | bytes 3145736 | tf_op jit(solution)/shard_map/ppermute | solution.py:15
  71.8 6.8 %collective-permute-start.2 = (f32[2048,128]{0,1:T(8,128)}, f32[2048,128]{0,1:T(8,128)S(1)}, u32[]{:S(2)}, u32[]{:S(2)}) collective-permute-start(f32[2048,128]{0,1:T(8,128)} %pad_maximum_fusion.2), channel_id=1, source_target_pairs={{0,1},{1,0},{2,3},{3,2},{4,5},{5,4},{6,7},{7,6},{8,9},{9,8},{10,11... | collective-permute-start | bytes 3145736 | tf_op jit(solution)/shard_map/ppermute | solution.py:15
  83.7 26.5 %collective-permute-start.3 = (f32[2048,128]{0,1:T(8,128)}, f32[2048,128]{0,1:T(8,128)S(1)}, u32[]{:S(2)}, u32[]{:S(2)}) collective-permute-start(f32[2048,128]{0,1:T(8,128)} %pad_maximum_fusion.3), channel_id=1, source_target_pairs={{0,8},{1,9},{2,10},{3,11},{4,12},{5,13},{6,14},{7,15},{8,0},{9,1},... | collective-permute-start | bytes 3145736 | tf_op jit(solution)/shard_map/ppermute | solution.py:15
  87.0 24.9 %copy-start.2 = (f32[128,1024]{1,0:T(8,128)S(1)}, f32[128,1024]{1,0:T(8,128)}, u32[]{:S(2)}) copy-start(f32[128,1024]{1,0:T(8,128)} %param.11) | copy-start | bytes 1572868
where the time goes:
time: 121 us; the launch traced here: 120 us
  waiting for transfers between devices  58.1 us (48%)
  matrix products  24.8 us (20%)
  starting transfers between devices  21.5 us (18%)
  other arithmetic  13.3 us (11%)
  local copies, waits for them, and re-layouts  2.21 us (2%)
    ppermute x4, waiting for transfers between devices, partner(): return lax.ppermute(value, axis, pairs)  58.1 us
    ppermute x4, starting transfers between devices, partner(): return lax.ppermute(value, axis, pairs)  21.5 us
    sub x4, other arithmetic, rotate(): real_part * cosine - imag_part * sine  9.16 us
    dot_general x1, matrix products, shards(): jnp.matmul(weights, target_map, precision=HIGH).astype(jnp.bfloat16)  8.2 us
    dot_general x4, matrix products, shards(): jnp.matmul(received, other_matrix, precision=HIGH)  7.95 us
    dot_general x4, matrix products, shards(): jnp.matmul(rotated, own_matrix, precision=HIGH)  6.72 us
    concatenate x4, other arithmetic, rotate(): jnp.concatenate([real_part * cosine - imag_part * sine, real_part * sine...  4.17 us
  transfers between devices with their start and end apart: 4, of which 4 were waited for; matrix products, arithmetic and copies ran while one was open for 6% of the time, Pallas kernels for 0%

commit v1 on v0

v1 whole, which is shorter than its diff:
```python
import functools
import math

import jax
import jax.numpy as jnp
from jax import lax
from jax.experimental import pallas as pl
from jax.experimental.pallas import tpu as pltpu
from jax.sharding import PartitionSpec as P

MESH = pl.DeviceIdType.MESH
LANES = 128
HALF = 64
GROUP = 8
CHUNKS = 8
F32 = jnp.float32
BF16 = jnp.bfloat16


def sine_coefficients(terms):
    import numpy as np

    points = 0.5 * np.cos((np.arange(2000) + 0.5) / 2000 * np.pi / 2)
    basis = np.stack([points ** (2 * k + 1) for k in range(terms)], axis=1)
    solved = np.linalg.lstsq(basis, np.sin(2 * np.pi * points), rcond=None)[0]
    return [float(value) for value in solved]


SINE = sine_coefficients(7)


def split(value):
    high = value.astype(BF16)
    return high, (value - high.astype(F32)).astype(BF16)


def dot(left, right):
    return jnp.dot(left, right, preferred_element_type=F32)


def phase_tables(speed, turns):
    lane = lax.broadcasted_iota(jnp.int32, speed.shape, 1)
    first = lane < HALF
    angle = speed * turns + jnp.where(first, 0.25, 0.0)
    rest = angle - jnp.round(angle)
    square = rest * rest
    total = jnp.full_like(rest, SINE[-1])
    for term in SINE[-2::-1]:
        total = total * square + term
    wave = total * rest
    turned = pltpu.roll(wave, HALF, 1)
    return jnp.where(first, wave, turned), jnp.where(first, -turned, wave)


def rotate(weights, cosine, sine):
    return weights * cosine + pltpu.roll(weights, HALF, 1) * sine


def butterfly_kernel(
    rows, charges_hbm, speed_hbm, omega_hbm, mixers_hbm, source_hbm, out_hbm,
    charges, speed, omega, mixers, source, speeds, source_pair, first_pair, high_mix, low_mix,
    own_cos, own_sin, cos_tables, sin_tables, z_send, z_recv, a_send, a_recv, b_send,
    load_sem, speed_sems, z_send_sems, z_recv_sems, a_send_sem, a_recv_sems, b_send_sem, b_recv_sem, own_sem,
):
    block = rows // GROUP // CHUNKS
    per_peer = rows // GROUP
    bx, by = lax.axis_index("bx"), lax.axis_index("by")
    z_count = lax.axis_size("bx") // 2
    y_count = lax.axis_size("by") // 2
    side = lax.rem(bx, 2)
    x_hi, x_lo, core = bx // z_count, by // y_count, lax.rem(by, 2)
    me = x_hi * 4 + core * 2 + x_lo

    loads = [
        pltpu.make_async_copy(speed_hbm, speed, load_sem.at[0]),
        pltpu.make_async_copy(omega_hbm, omega, load_sem.at[1]),
        pltpu.make_async_copy(charges_hbm, charges, load_sem.at[2]),
        pltpu.make_async_copy(source_hbm, source, load_sem.at[3]),
        pltpu.make_async_copy(mixers_hbm, mixers, load_sem.at[4]),
    ]
    for load in loads:
        load.start()

    z_peer = {"bx": bx + 1 - 2 * side}
    peers = []
    for mask in range(1, GROUP):
        other_hi = lax.rem(x_hi + mask // 4, 2)
        other_core = lax.rem(core + mask // 2 % 2, 2)
        other_lo = lax.rem(x_lo + mask % 2, 2)
        device = {
            "bx": other_hi * z_count + lax.rem(bx, z_count),
            "by": other_lo * y_count + (lax.rem(by, y_count) // 2) * 2 + other_core,
        }
        peers.append((device, other_hi * 4 + other_core * 2 + other_lo))

    barrier = pltpu.get_barrier_semaphore()
    pl.semaphore_signal(barrier, inc=1, device_id=z_peer, device_id_type=MESH)
    for device, _ in peers:
        pl.semaphore_signal(barrier, inc=1, device_id=device, device_id_type=MESH)

    def column(row):
        return jnp.transpose(jnp.broadcast_to(row, (LANES, LANES)))

    halves = per_peer // LANES
    loads[0].wait()
    loads[1].wait()

    def turns_of(level):
        return omega[pl.ds(level, 1), :] * (1.0 / (2.0 * math.pi))

    def own_tables(step, carry):
        half, place = step // GROUP, lax.rem(step, GROUP)
        cosine, sine = phase_tables(column(speed[place, pl.ds(half, 1), :]), turns_of(0))
        span = pl.ds(pl.multiple_of(half * LANES, LANES), LANES)
        own_cos[place, span, :] = cosine
        own_sin[place, span, :] = sine
        return carry

    lax.fori_loop(0, halves * GROUP, own_tables, 0)

    loads[3].wait()
    high, low = split(source[...])
    source_pair[0:LANES, 0:LANES] = high
    source_pair[0:LANES, LANES:] = low
    source_pair[LANES:, 0:LANES] = high
    source_pair[LANES:, LANES:] = jnp.zeros_like(high)
    loads[2].wait()

    def span_of(chunk):
        return pl.ds(pl.multiple_of(chunk * block, block), block)

    def start(chunk):
        span = span_of(chunk)
        high, low = split(charges[:, span, :].reshape(GROUP * block, LANES))
        both = dot(jnp.concatenate([high, low], axis=1), source_pair[...])
        weights = both[:, :LANES] + both[:, LANES:]
        cosine = own_cos[:, span, :].reshape(GROUP * block, LANES)
        sine = own_sin[:, span, :].reshape(GROUP * block, LANES)
        z_send[chunk] = rotate(weights, cosine, sine).reshape(GROUP, block, LANES)

    def z_copy(chunk):
        return pltpu.make_async_remote_copy(
            src_ref=z_send.at[chunk], dst_ref=z_recv.at[chunk],
            send_sem=z_send_sems.at[chunk], recv_sem=z_recv_sems.at[chunk],
            device_id=z_peer, device_id_type=MESH,
        )

    start(0)
    pl.semaphore_wait(barrier, GROUP)
    z_copy(0).start()
    for device, place in peers:
        pltpu.make_async_remote_copy(
            src_ref=speed.at[place], dst_ref=speeds.at[me],
            send_sem=speed_sems.at[0], recv_sem=speed_sems.at[1],
            device_id=device, device_id_type=MESH,
        ).start()

    def start_and_send(chunk, carry):
        start(chunk)
        z_copy(chunk).start()
        return carry

    lax.fori_loop(1, CHUNKS, start_and_send, 0)

    loads[4].wait()
    for child in range(2):
        high, low = split(mixers[0, side, lax.rem(side + child, 2)])
        first_pair[child * LANES:(child + 1) * LANES, 0:LANES] = high
        first_pair[child * LANES:(child + 1) * LANES, LANES:] = low
        for level in range(1, 4):
            for target in range(2):
                high, low = split(mixers[level, target, child])
                place = (level - 1, slice(child * LANES, (child + 1) * LANES), slice(target * LANES, (target + 1) * LANES))
                high_mix[place] = high
                low_mix[place] = low

    def wait_bytes(ref, sem):
        pltpu.make_async_copy(ref, ref, sem).wait()

    speeds[me] = speed[me]
    wait_bytes(speeds.at[pl.ds(0, GROUP - 1)], speed_sems.at[1])

    def group_tables(step, carry):
        half, place = step // GROUP, lax.rem(step, GROUP)
        wide = column(speeds[place, pl.ds(half, 1), :])
        span = pl.ds(pl.multiple_of(half * LANES, LANES), LANES)
        for level in range(1, 4):
            cosine, sine = phase_tables(wide, turns_of(level))
            cos_tables[level - 1, place, span, :] = cosine
            sin_tables[level - 1, place, span, :] = sine
        return carry

    lax.fori_loop(0, halves * GROUP, group_tables, 0)

    def first_level(chunk):
        z_copy(chunk).wait_recv()
        own = z_send[chunk].reshape(GROUP * block, LANES)
        other = z_recv[chunk].reshape(GROUP * block, LANES)
        high, low = split(jnp.concatenate([own, other], axis=1))
        both = dot(high, first_pair[...])
        total = both[:, :LANES] + both[:, LANES:] + dot(low, first_pair[:, :LANES])
        a_send[chunk] = total.reshape(GROUP, block, LANES)
        for device, place in peers:
            pltpu.make_async_remote_copy(
                src_ref=a_send.at[chunk, place], dst_ref=a_recv.at[chunk, me],
                send_sem=a_send_sem, recv_sem=a_recv_sems.at[chunk],
                device_id=device, device_id_type=MESH,
            ).start()
        a_recv[chunk, me] = a_send[chunk, me]

    def other_levels(chunk):
        wait_bytes(a_recv.at[chunk, pl.ds(0, GROUP - 1)], a_recv_sems.at[chunk])
        span = span_of(chunk)
        weights = a_recv[chunk].reshape(GROUP * block, LANES)
        for level in range(1, 4):
            cosine = cos_tables[level - 1, :, span, :].reshape(GROUP * block, LANES)
            sine = sin_tables[level - 1, :, span, :].reshape(GROUP * block, LANES)
            rotated = rotate(weights, cosine, sine)
            stride = {1: 4, 2: 2, 3: 1}[level]
            low_places = [place for place in range(GROUP) if place // stride % 2 == 0]

            def rows_of(place):
                return rotated[place * block:(place + 1) * block]

            pairs = jnp.concatenate(
                [
                    jnp.concatenate([rows_of(place) for place in low_places], axis=0),
                    jnp.concatenate([rows_of(place + stride) for place in low_places], axis=0),
                ],
                axis=1,
            )
            high, low = split(pairs)
            both = dot(jnp.concatenate([high, low], axis=0), high_mix[level - 1])
            count = pairs.shape[0]
            mixed = both[:count] + both[count:] + dot(high, low_mix[level - 1])
            parts = [None] * GROUP
            for index, place in enumerate(low_places):
                taken = mixed[index * block:(index + 1) * block]
                parts[place] = taken[:, :LANES]
                parts[place + stride] = taken[:, LANES:]
            weights = jnp.concatenate(parts, axis=0)
        b_send[chunk] = weights.reshape(GROUP, block, LANES)
        for device, place in peers:
            pltpu.make_async_remote_copy(
                src_ref=b_send.at[chunk, place], dst_ref=out_hbm.at[me, span],
                send_sem=b_send_sem, recv_sem=b_recv_sem,
                device_id=device, device_id_type=MESH,
            ).start()
        pltpu.make_async_copy(b_send.at[chunk, me], out_hbm.at[me, span], own_sem).start()

    def step(index, carry):
        @pl.when(index < CHUNKS)
        def _():
            first_level(index)

        @pl.when(index > 0)
        def _():
            other_levels(index - 1)

        return carry

    lax.fori_loop(0, CHUNKS + 1, step, 0)

    wait_bytes(out_hbm.at[pl.ds(0, GROUP - 1)], b_recv_sem)
    wait_bytes(out_hbm.at[0], own_sem)
    wait_bytes(out_hbm.at[pl.ds(0, GROUP - 1)], a_send_sem)
    wait_bytes(out_hbm.at[pl.ds(0, GROUP - 1)], b_send_sem)
    wait_bytes(speeds.at[pl.ds(0, GROUP - 1)], speed_sems.at[0])
    for chunk in range(CHUNKS):
        z_copy(chunk).wait_send()


def butterfly(charges, speed, omega, mixers, source_map):
    rows = charges.shape[0]
    per_peer = rows // GROUP
    block = per_peer // CHUNKS
    chunked = (CHUNKS, GROUP, block, LANES)
    whole = (GROUP, per_peer, LANES)
    dma = pltpu.SemaphoreType.DMA
    return pl.pallas_call(
        functools.partial(butterfly_kernel, rows),
        name="butterfly",
        out_shape=jax.ShapeDtypeStruct(whole, F32),
        in_specs=[pl.BlockSpec(memory_space=pl.ANY)] * 5,
        out_specs=pl.BlockSpec(memory_space=pl.ANY),
        scratch_shapes=[
            pltpu.VMEM(whole, F32),
            pltpu.VMEM((GROUP, per_peer // LANES, LANES), F32),
            pltpu.VMEM((4, LANES), F32),
            pltpu.VMEM((4, 2, 2, LANES, LANES), F32),
            pltpu.VMEM((LANES, LANES), F32),
            pltpu.VMEM((GROUP, per_peer // LANES, LANES), F32),
            pltpu.VMEM((2 * LANES, 2 * LANES), BF16),
            pltpu.VMEM((2 * LANES, 2 * LANES), BF16),
            pltpu.VMEM((3, 2 * LANES, 2 * LANES), BF16),
            pltpu.VMEM((3, 2 * LANES, 2 * LANES), BF16),
            pltpu.VMEM(whole, F32),
            pltpu.VMEM(whole, F32),
            pltpu.VMEM((3,) + whole, F32),
            pltpu.VMEM((3,) + whole, F32),
            pltpu.VMEM(chunked, F32),
            pltpu.VMEM(chunked, F32),
            pltpu.VMEM(chunked, F32),
            pltpu.VMEM(chunked, F32),
            pltpu.VMEM(chunked, F32),
            dma((5,)),
            dma((2,)),
            dma((CHUNKS,)),
            dma((CHUNKS,)),
            dma,
            dma((CHUNKS,)),
            dma,
            dma,
            dma,
        ],
        compiler_params=pltpu.CompilerParams(
            collective_id=0, has_side_effects=True, vmem_limit_bytes=32 * 2**20
        ),
    )(
        charges.reshape(whole),
        speed.reshape(GROUP, per_peer // LANES, LANES),
        jnp.concatenate([omega, omega], axis=1),
        mixers,
        source_map,
    )


def target_kernel(weights_ref, map_ref, out_ref, double, lower):
    @pl.when(pl.program_id(0) == 0)
    def _():
        high, low = split(map_ref[...])
        double[0:LANES, :] = high
        double[LANES:, :] = high
        lower[...] = low

    high, low = split(weights_ref[...])
    total = dot(jnp.concatenate([high, low], axis=1), double[...]) + dot(high, lower[...])
    out_ref[...] = total.astype(BF16)


def apply_target(weights, target_map):
    rows, targets = weights.shape[0], target_map.shape[1]
    tile = rows // 8
    return pl.pallas_call(
        target_kernel,
        name="target",
        grid=(rows // tile,),
        out_shape=jax.ShapeDtypeStruct((rows, targets), BF16),
        in_specs=[
            pl.BlockSpec((tile, LANES), lambda i: (i, 0)),
            pl.BlockSpec((LANES, targets), lambda i: (0, 0)),
        ],
        out_specs=pl.BlockSpec((tile, targets), lambda i: (i, 0)),
        scratch_shapes=[pltpu.VMEM((2 * LANES, targets), BF16), pltpu.VMEM((LANES, targets), BF16)],
        compiler_params=pltpu.CompilerParams(vmem_limit_bytes=24 * 2**20),
    )(weights, target_map)


def shards(charges, speed, omega, mixers, source_map, target_map):
    box_count = charges.shape[2]
    weights = butterfly(
        charges.reshape(box_count, charges.shape[3]), speed, omega, mixers, source_map
    )
    result = apply_target(weights.reshape(box_count, LANES), target_map)
    return result.reshape(1, 1, box_count, target_map.shape[1])


def solution(mesh):
    placed = (P("bx", "by", None, None), P("bx", "by", None), P(), P(), P(), P())
    return jax.shard_map(
        shards, mesh=mesh, in_specs=placed, out_specs=P("bx", "by", None, None), check_vma=False
    )
```

time: 121 us -> 61.7 us (0.51)
  waiting for transfers between devices: 58.1 us -> 0 us
  Pallas kernels: 0 us -> 55.5 us
  matrix products: 24.8 us -> 0 us
  starting transfers between devices: 21.5 us -> 0 us
  other arithmetic: 13.3 us -> 0.83 us
  local copies, waits for them, and re-layouts: 2.21 us -> 5.02 us
    ppermute x4 -> x0, waiting for transfers between devices: 58.1 us -> none  [partner(): return lax.ppermute(value, axis, pairs)]
    pallas_call x0 -> x2, Pallas kernels: none -> 55.5 us  [the longest x1 50.1 us: butterfly(): pl.pallas_call(functools.partial(butterfly_kernel, rows), name='butterfly...]
    dot_general x10 -> x0, matrix products: 24.8 us -> none  [the longest x1 8.2 us: shards(): jnp.matmul(weights, target_map, precision=HIGH).astype(jnp.bfloat16)]
    ppermute x4 -> x0, starting transfers between devices: 21.5 us -> none  [partner(): return lax.ppermute(value, axis, pairs)]
    sub x4 -> x0, other arithmetic: 9.16 us -> none  [rotate(): real_part * cosine - imag_part * sine]
    unnamed x8 -> x10, local copies, waits for them, and re-layouts: 0.42 us -> 5.02 us
    concatenate x4 -> x1, other arithmetic: 4.17 us -> 0.83 us  [butterfly(): jnp.concatenate([omega, omega], axis=1)]
  transfers between devices with their start and end apart: 4 -> 0, of which waited for: 4 -> 0; matrix products, arithmetic and copies ran while one was open for 6% -> 0% of each run, Pallas kernels for 0% -> 0%
where the time goes in v1:
time: 61.7 us; the launch traced here: 61.3 us
  Pallas kernels  55.5 us (90%)
  local copies, waits for them, and re-layouts  5.02 us (8%)
  other arithmetic  0.83 us (1%)
    pallas_call x1, Pallas kernels, butterfly(): pl.pallas_call(functools.partial(butterfly_kernel, rows), name='butterfly...  50.1 us
    pallas_call x1, Pallas kernels, apply_target(): pl.pallas_call(target_kernel, name='target', grid=(rows // tile,), out_sh...  5.4 us
    unnamed x10, local copies, waits for them, and re-layouts  5.02 us

profile of v1, /device:TPU:1, one launch (start us, length us, event | category | flops | bytes accessed | tf_op | source)
XLA Modules:
  0.0 61.3 jit_solution(4288552601020668686)
XLA Ops:
  0.0 0.8 %pad_maximum_fusion.omega_hbm = f32[4,128]{1,0:T(4,128)S(1)} fusion(f32[4,64]{1,0:T(4,128)} %param.8), kind=kLoop, calls=%fused_computation | loop fusion | flops 512 | bytes 3072 | tf_op jit(solution)/shard_map/concatenate | solution.py:322
  0.8 0.0 copy-start
  0.8 1.2 %copy-done = f32[1,1,2048,128]{3,2,1,0:T(8,128)S(1)} copy-done((f32[1,1,2048,128]{3,2,1,0:T(8,128)S(1)}, f32[1,1,2048,128]{3,2,1,0:T(8,128)}, u32[]{:S(2)}) %copy-start) | copy-done | bytes 1048600
  2.1 0.0 copy-start.1
  2.1 1.2 %copy-done.1 = f32[4,2,2,128,128]{4,3,2,1,0:T(8,128)S(1)} copy-done((f32[4,2,2,128,128]{4,3,2,1,0:T(8,128)S(1)}, f32[4,2,2,128,128]{4,3,2,1,0:T(8,128)}, u32[]{:S(2)}) %copy-start.1) | copy-done | bytes 1048600
  3.3 0.0 copy-start.3
  3.3 0.8 %copy-done.3 = f32[128,128]{1,0:T(8,128)S(1)} copy-done((f32[128,128]{1,0:T(8,128)S(1)}, f32[128,128]{1,0:T(8,128)}, u32[]{:S(2)}) %copy-start.3) | copy-done | bytes 65560
  4.1 0.0 copy-start.4
  4.1 0.7 %copy-done.4 = f32[1,1,2048]{2,1,0:T(1,128)S(1)} copy-done((f32[1,1,2048]{2,1,0:T(1,128)S(1)}, f32[1,1,2048]{2,1,0:T(1,128)}, u32[]{:S(2)}) %copy-start.4) | copy-done | bytes 8216
  4.8 50.1 %butterfly.1 = f32[8,256,128]{2,1,0:T(8,128)S(1)} custom-call(f32[8,256,128]{2,1,0:T(8,128)S(1)} %bitcast.5, f32[8,2,128]{2,1,0:T(2,128)S(1)} %bitcast.6, f32[4,128]{1,0:T(4,128)S(1)} %pad_maximum_fusion.omega_hbm, f32[4,2,2,128,128]{4,3,2,1,0:T(8,128)S(1)} %copy-done.1, f32[128,128]{1,0:T(8,128)S(1)} %copy-done.3), custom_call_target="tpu_custom_call" | custom-call | tf_op jit(solution)/shard_map/butterfly/pallas_call | solution.py:280
  54.9 0.0 copy-start.2
  54.9 1.0 %copy-done.2 = f32[128,1024]{1,0:T(8,128)S(1)} copy-done((f32[128,1024]{1,0:T(8,128)S(1)}, f32[128,1024]{1,0:T(8,128)}, u32[]{:S(2)}) %copy-start.2) | copy-done | bytes 524312
  55.9 5.4 %target.1 = bf16[2048,1024]{1,0:T(8,128)(2,1)} custom-call(f32[2048,128]{1,0:T(8,128)S(1)} %bitcast.4, f32[128,1024]{1,0:T(8,128)S(1)} %copy-done.2), custom_call_target="tpu_custom_call" | custom-call | tf_op jit(solution)/shard_map/target/pallas_call | solution.py:344
Async XLA Ops:
  0.8 1.2 %copy-start = (f32[1,1,2048,128]{3,2,1,0:T(8,128)S(1)}, f32[1,1,2048,128]{3,2,1,0:T(8,128)}, u32[]{:S(2)}) copy-start(f32[1,1,2048,128]{3,2,1,0:T(8,128)} %param.6) | copy-start | bytes 3145732
  2.1 1.2 %copy-start.1 = (f32[4,2,2,128,128]{4,3,2,1,0:T(8,128)S(1)}, f32[4,2,2,128,128]{4,3,2,1,0:T(8,128)}, u32[]{:S(2)}) copy-start(f32[4,2,2,128,128]{4,3,2,1,0:T(8,128)} %mixers_hbm.1) | copy-start | bytes 3145732
  3.3 0.8 %copy-start.3 = (f32[128,128]{1,0:T(8,128)S(1)}, f32[128,128]{1,0:T(8,128)}, u32[]{:S(2)}) copy-start(f32[128,128]{1,0:T(8,128)} %source_hbm.1) | copy-start | bytes 196612
  4.1 0.7 %copy-start.4 = (f32[1,1,2048]{2,1,0:T(1,128)S(1)}, f32[1,1,2048]{2,1,0:T(1,128)}, u32[]{:S(2)}) copy-start(f32[1,1,2048]{2,1,0:T(1,128)} %param.7) | copy-start | bytes 24580
  54.9 1.0 %copy-start.2 = (f32[128,1024]{1,0:T(8,128)S(1)}, f32[128,1024]{1,0:T(8,128)}, u32[]{:S(2)}) copy-start(f32[128,1024]{1,0:T(8,128)} %map_ref.1) | copy-start | bytes 1572868

commit v2 on v1

v2 whole, which is shorter than its diff:
```python
import functools
import math

import jax
import jax.numpy as jnp
from jax import lax
from jax.experimental import pallas as pl
from jax.experimental.pallas import tpu as pltpu
from jax.sharding import PartitionSpec as P

MESH = pl.DeviceIdType.MESH
LANES = 128
HALF = 64
GROUP = 8
CHUNKS = 8
Z_FIRST = 2
Z_END = CHUNKS // 2
PEER_ORDER = (1, 5, 4, 3, 7, 6, 2)
VMEM_LIMIT = 60 * 2**20
F32 = jnp.float32
BF16 = jnp.bfloat16


def sine_coefficients(terms):
    import numpy as np

    points = 0.5 * np.cos((np.arange(2000) + 0.5) / 2000 * np.pi / 2)
    basis = np.stack([points ** (2 * k + 1) for k in range(terms)], axis=1)
    solved = np.linalg.lstsq(basis, np.sin(2 * np.pi * points), rcond=None)[0]
    return [float(value) for value in solved]


SINE = sine_coefficients(7)


def split(value):
    high = value.astype(BF16)
    return high, (value - high.astype(F32)).astype(BF16)


def dot(left, right):
    return jnp.dot(left, right, preferred_element_type=F32)


def phase_tables(speed, turns):
    lane = lax.broadcasted_iota(jnp.int32, speed.shape, 1)
    first = lane < HALF
    angle = speed * turns + jnp.where(first, 0.25, 0.0)
    rest = angle - jnp.round(angle)
    square = rest * rest
    total = jnp.full_like(rest, SINE[-1])
    for term in SINE[-2::-1]:
        total = total * square + term
    wave = total * rest
    turned = pltpu.roll(wave, HALF, 1)
    return jnp.where(first, wave, turned), jnp.where(first, -turned, wave)


def rotate(weights, cosine, sine):
    return weights * cosine + pltpu.roll(weights, HALF, 1) * sine


def butterfly_kernel(
    rows, charges_hbm, speed_hbm, omega_hbm, mixers_hbm, source_hbm, out_ref,
    charges, speed, omega, mixers, source, speeds, wide, source_pair, first_pair, high_mix, low_mix,
    tables, z_send, z_recv, a_send, a_recv, b_send,
    load_sems, speed_sems, z_send_sems, z_recv_sems, a_send_sem, a_recv_sems, b_send_sem, b_recv_sem,
):
    per_peer = rows // GROUP
    block = per_peer // CHUNKS
    count = GROUP * block
    bx, by = lax.axis_index("bx"), lax.axis_index("by")
    z_count = lax.axis_size("bx") // 2
    y_count = lax.axis_size("by") // 2
    side = lax.rem(bx, 2)
    x_hi, x_lo, core = bx // z_count, by // y_count, lax.rem(by, 2)
    me = x_hi * 4 + core * 2 + x_lo

    z_peer = {"bx": bx + 1 - 2 * side}
    peers = []
    for mask in PEER_ORDER:
        other_hi = lax.rem(x_hi + mask // 4, 2)
        other_core = lax.rem(core + mask // 2 % 2, 2)
        other_lo = lax.rem(x_lo + mask % 2, 2)
        device = {
            "bx": other_hi * z_count + lax.rem(bx, z_count),
            "by": other_lo * y_count + (lax.rem(by, y_count) // 2) * 2 + other_core,
        }
        peers.append((device, other_hi * 4 + other_core * 2 + other_lo))

    barrier = pltpu.get_barrier_semaphore()
    for device, _ in peers[::-1]:
        pl.semaphore_signal(barrier, inc=1, device_id=device, device_id_type=MESH)
    pl.semaphore_signal(barrier, inc=1, device_id=z_peer, device_id_type=MESH)

    loads = [
        pltpu.make_async_copy(speed_hbm, speed, load_sems.at[0]),
        pltpu.make_async_copy(omega_hbm, omega, load_sems.at[1]),
        pltpu.make_async_copy(source_hbm, source, load_sems.at[2]),
        pltpu.make_async_copy(charges_hbm.at[:, pl.ds(0, Z_FIRST * block)], charges, load_sems.at[3]),
        pltpu.make_async_copy(mixers_hbm, mixers, load_sems.at[4]),
    ]
    for load in loads:
        load.start()

    def wait_bytes(ref, sem):
        pltpu.make_async_copy(ref, ref, sem).wait()

    def span_of(chunk):
        return pl.ds(pl.multiple_of(chunk * block, block), block)

    def turns_of(level):
        row = omega[pl.ds(level, 1), :] * (1.0 / (2.0 * math.pi))
        return jnp.concatenate([row, row], axis=1)

    def source_weights(value):
        high, low = split(value)
        both = dot(jnp.concatenate([high, low], axis=1), source_pair[...])
        return both[:, :LANES] + both[:, LANES:]

    def z_copy(chunk):
        return pltpu.make_async_remote_copy(
            src_ref=z_send.at[chunk], dst_ref=z_recv.at[chunk],
            send_sem=z_send_sems.at[chunk], recv_sem=z_recv_sems.at[chunk],
            device_id=z_peer, device_id_type=MESH,
        )

    def scatter(block_of, chunk):
        for device, place in peers:
            pltpu.make_async_remote_copy(
                src_ref=block_of(place), dst_ref=a_recv.at[chunk, me],
                send_sem=a_send_sem, recv_sem=a_recv_sems.at[chunk],
                device_id=device, device_id_type=MESH,
            ).start()
        pltpu.make_async_copy(block_of(me), a_recv.at[chunk, me], a_recv_sems.at[chunk]).start()

    def give_back(chunk):
        span = span_of(chunk)
        for device, place in peers:
            pltpu.make_async_remote_copy(
                src_ref=b_send.at[chunk, place], dst_ref=out_ref.at[me, span],
                send_sem=b_send_sem, recv_sem=b_recv_sem,
                device_id=device, device_id_type=MESH,
            ).start()
        pltpu.make_async_copy(b_send.at[chunk, me], out_ref.at[me, span], b_recv_sem).start()

    loads[0].wait()
    columns = jnp.transpose(speed[:, 0, :])
    own_speed = [
        jnp.concatenate(
            [
                jnp.broadcast_to(columns[chunk * block:(chunk + 1) * block, place:place + 1], (block, LANES))
                for place in range(GROUP)
            ],
            axis=0,
        )
        for chunk in range(Z_FIRST)
    ]
    loads[1].wait()
    loads[2].wait()
    high, low = split(source[...])
    source_pair[0:LANES, 0:LANES] = high
    source_pair[0:LANES, LANES:] = low
    source_pair[LANES:, 0:LANES] = high
    source_pair[LANES:, LANES:] = jnp.zeros_like(high)
    loads[3].wait()
    for chunk in range(Z_FIRST):
        cosine, sine = phase_tables(own_speed[chunk], turns_of(0))
        weights = source_weights(charges[:, chunk * block:(chunk + 1) * block, :].reshape(count, LANES))
        z_send[chunk] = rotate(weights, cosine, sine).reshape(GROUP, block, LANES)
        if chunk == 0:
            pl.semaphore_wait(barrier, GROUP)
            z_copy(0).start()
            for device, place in peers:
                pltpu.make_async_remote_copy(
                    src_ref=speed.at[place], dst_ref=speeds.at[me],
                    send_sem=speed_sems.at[0], recv_sem=speed_sems.at[1],
                    device_id=device, device_id_type=MESH,
                ).start()

            def scatter_charges(later, carry):
                scatter(lambda place: charges_hbm.at[place, span_of(later)], later)
                return carry

            lax.fori_loop(Z_FIRST, CHUNKS, scatter_charges, 0)
        else:
            z_copy(chunk).start()

    speeds[me] = speed[me]
    loads[4].wait()
    for child in range(2):
        high, low = split(mixers[0, side, lax.rem(side + child, 2)])
        first_pair[child * LANES:(child + 1) * LANES, 0:LANES] = high
        first_pair[child * LANES:(child + 1) * LANES, LANES:] = low
        for level in range(1, 4):
            for target in range(2):
                high, low = split(mixers[level, target, child])
                place = (level - 1, slice(child * LANES, (child + 1) * LANES), slice(target * LANES, (target + 1) * LANES))
                high_mix[place] = high
                low_mix[place] = low

    wait_bytes(speeds.at[pl.ds(0, GROUP - 1)], speed_sems.at[1])
    for half in range(per_peer // LANES):
        columns = jnp.transpose(speeds[:, half, :])
        for place in range(GROUP):
            wide[place, half * LANES:(half + 1) * LANES, :] = jnp.broadcast_to(
                columns[:, place:place + 1], (LANES, LANES)
            )

    def make_tables(chunk):
        speed_here = wide[:, span_of(chunk), :].reshape(count, LANES)
        for level in range(1, 4):
            cosine, sine = phase_tables(speed_here, turns_of(level))
            tables[chunk, level - 1, 0] = cosine
            tables[chunk, level - 1, 1] = sine

    def first_level(chunk):
        own = z_send[chunk].reshape(count, LANES)
        other = z_recv[chunk].reshape(count, LANES)
        high, low = split(jnp.concatenate([own, other], axis=1))
        both = dot(high, first_pair[...])
        return both[:, :LANES] + both[:, LANES:] + dot(low, first_pair[:, :LANES])

    def other_levels(chunk, weights):
        for level in range(1, 4):
            rotated = rotate(weights, tables[chunk, level - 1, 0], tables[chunk, level - 1, 1])
            stride = {1: 4, 2: 2, 3: 1}[level]
            low_places = [place for place in range(GROUP) if place // stride % 2 == 0]

            def rows_of(place):
                return rotated[place * block:(place + 1) * block]

            pairs = jnp.concatenate(
                [
                    jnp.concatenate([rows_of(place) for place in low_places], axis=0),
                    jnp.concatenate([rows_of(place + stride) for place in low_places], axis=0),
                ],
                axis=1,
            )
            high, low = split(pairs)
            both = dot(jnp.concatenate([high, low], axis=0), high_mix[level - 1])
            half = count // 2
            mixed = both[:half] + both[half:] + dot(high, low_mix[level - 1])
            parts = [None] * GROUP
            for index, place in enumerate(low_places):
                taken = mixed[index * block:(index + 1) * block]
                parts[place] = taken[:, :LANES]
                parts[place + stride] = taken[:, LANES:]
            weights = jnp.concatenate(parts, axis=0)
        b_send[chunk] = weights.reshape(GROUP, block, LANES)
        give_back(chunk)

    def x_first_start(chunk):
        speed_here = wide[:, span_of(chunk), :].reshape(count, LANES)
        cosine, sine = phase_tables(speed_here, turns_of(0))
        wait_bytes(a_recv.at[chunk], a_recv_sems.at[chunk])
        weights = source_weights(a_recv[chunk].reshape(count, LANES))
        z_send[chunk] = rotate(weights, cosine, sine).reshape(GROUP, block, LANES)
        z_copy(chunk).start()
        make_tables(chunk)

    def z_first_middle(chunk):
        z_copy(chunk).wait_recv()
        a_send[chunk] = first_level(chunk).reshape(GROUP, block, LANES)
        scatter(lambda place: a_send.at[chunk, place], chunk)

    def z_first_end(chunk):
        wait_bytes(a_recv.at[chunk], a_recv_sems.at[chunk])
        other_levels(chunk, a_recv[chunk].reshape(count, LANES))

    def x_first_end(chunk):
        z_copy(chunk).wait_recv()
        other_levels(chunk, first_level(chunk))

    def early(chunk, carry):
        x_first_start(chunk + Z_FIRST)
        z_first_middle(chunk)
        make_tables(chunk)
        return carry

    def late(chunk, carry):
        @pl.when(chunk < CHUNKS - Z_FIRST)
        def _():
            x_first_start(chunk + Z_FIRST)

        x_first_end(chunk)

        @pl.when((chunk >= Z_END) & (chunk < Z_END + Z_FIRST))
        def _():
            z_first_end(chunk - Z_END)

        return carry

    lax.fori_loop(0, Z_FIRST, early, 0)
    lax.fori_loop(Z_FIRST, CHUNKS, late, 0)

    wait_bytes(out_ref, b_recv_sem)
    most = out_ref.at[pl.ds(0, GROUP - 1)]
    wait_bytes(most, a_send_sem)
    wait_bytes(most, b_send_sem)
    wait_bytes(speeds.at[pl.ds(0, GROUP - 1)], speed_sems.at[0])
    for chunk in range(CHUNKS):
        z_copy(chunk).wait_send()


def butterfly(charges, speed, omega, mixers, source_map):
    rows = charges.shape[0]
    per_peer = rows // GROUP
    block = per_peer // CHUNKS
    chunked = (CHUNKS, GROUP, block, LANES)
    whole = (GROUP, per_peer, LANES)
    lines = (GROUP, per_peer // LANES, LANES)
    dma = pltpu.SemaphoreType.DMA
    return pl.pallas_call(
        functools.partial(butterfly_kernel, rows),
        name="butterfly",
        out_shape=jax.ShapeDtypeStruct(whole, F32),
        in_specs=[pl.BlockSpec(memory_space=pltpu.HBM)] * 5,
        out_specs=pl.BlockSpec(memory_space=pl.ANY),
        scratch_shapes=[
            pltpu.VMEM((GROUP, Z_FIRST * block, LANES), F32),
            pltpu.VMEM(lines, F32),
            pltpu.VMEM((4, HALF), F32),
            pltpu.VMEM((4, 2, 2, LANES, LANES), F32),
            pltpu.VMEM((LANES, LANES), F32),
            pltpu.VMEM(lines, F32),
            pltpu.VMEM(whole, F32),
            pltpu.VMEM((2 * LANES, 2 * LANES), BF16),
            pltpu.VMEM((2 * LANES, 2 * LANES), BF16),
            pltpu.VMEM((3, 2 * LANES, 2 * LANES), BF16),
            pltpu.VMEM((3, 2 * LANES, 2 * LANES), BF16),
            pltpu.VMEM((CHUNKS, 3, 2, GROUP * block, LANES), F32),
            pltpu.VMEM(chunked, F32),
            pltpu.VMEM(chunked, F32),
            pltpu.VMEM((Z_FIRST,) + chunked[1:], F32),
            pltpu.VMEM(chunked, F32),
            pltpu.VMEM(chunked, F32),
            dma((5,)),
            dma((2,)),
            dma((CHUNKS,)),
            dma((CHUNKS,)),
            dma,
            dma((CHUNKS,)),
            dma,
            dma,
        ],
        compiler_params=pltpu.CompilerParams(
            collective_id=0, has_side_effects=True, vmem_limit_bytes=VMEM_LIMIT
        ),
    )(
        charges.reshape(whole),
        speed.reshape(lines),
        omega,
        mixers,
        source_map,
    )


def target_kernel(weights_ref, map_ref, out_ref, double, lower):
    @pl.when(pl.program_id(0) == 0)
    def _():
        high, low = split(map_ref[...])
        double[0:LANES, :] = high
        double[LANES:, :] = high
        lower[...] = low

    high, low = split(weights_ref[...])
    total = dot(jnp.concatenate([high, low], axis=1), double[...]) + dot(high, lower[...])
    out_ref[...] = total.astype(BF16)


def apply_target(weights, target_map):
    rows, targets = weights.shape[0], target_map.shape[1]
    tile = rows // 8
    return pl.pallas_call(
        target_kernel,
        name="target",
        grid=(rows // tile,),
        out_shape=jax.ShapeDtypeStruct((rows, targets), BF16),
        in_specs=[
            pl.BlockSpec((tile, LANES), lambda i: (i, 0)),
            pl.BlockSpec((LANES, targets), lambda i: (0, 0)),
        ],
        out_specs=pl.BlockSpec((tile, targets), lambda i: (i, 0)),
        scratch_shapes=[pltpu.VMEM((2 * LANES, targets), BF16), pltpu.VMEM((LANES, targets), BF16)],
        compiler_params=pltpu.CompilerParams(vmem_limit_bytes=24 * 2**20),
    )(weights, target_map)


def shards(charges, speed, omega, mixers, source_map, target_map):
    box_count = charges.shape[2]
    weights = butterfly(
        charges.reshape(box_count, charges.shape[3]), speed, omega, mixers, source_map
    )
    result = apply_target(weights.reshape(box_count, LANES), target_map)
    return result.reshape(1, 1, box_count, target_map.shape[1])


def solution(mesh):
    placed = (P("bx", "by", None, None), P("bx", "by", None), P(), P(), P(), P())
    return jax.shard_map(
        shards, mesh=mesh, in_specs=placed, out_specs=P("bx", "by", None, None), check_vma=False
    )
```

time: 61.7 us -> 45.1 us (0.73)
  Pallas kernels: 55.5 us -> 42.7 us
  local copies, waits for them, and re-layouts: 5.02 us -> 2.26 us
  other arithmetic: 0.83 us -> 0 us
    pallas_call x1, Pallas kernels: 50.1 us -> 37.3 us  [butterfly(): pl.pallas_call(functools.partial(butterfly_kernel, rows), name='butterfly...]
    unnamed x10 -> x4, local copies, waits for them, and re-layouts: 5.02 us -> 2.26 us
    concatenate x1 -> x0, other arithmetic: 0.83 us -> none  [butterfly(): jnp.concatenate([omega, omega], axis=1)]
where the time goes in v2:
time: 45.1 us; the launch traced here: 44.9 us
  Pallas kernels  42.7 us (95%)
  local copies, waits for them, and re-layouts  2.26 us (5%)
    pallas_call x1, Pallas kernels, butterfly(): pl.pallas_call(functools.partial(butterfly_kernel, rows), name='butterfly...  37.3 us
    pallas_call x1, Pallas kernels, apply_target(): pl.pallas_call(target_kernel, name='target', grid=(rows // tile,), out_sh...  5.37 us
    unnamed x4, local copies, waits for them, and re-layouts  2.26 us

profile of v2, /device:TPU:1, one launch (start us, length us, event | category | flops | bytes accessed | tf_op | source)
XLA Modules:
  0.0 44.9 jit_solution(11266399127089781025)
XLA Ops:
  0.0 37.3 %butterfly.1 = f32[8,256,128]{2,1,0:T(8,128)} custom-call(f32[8,256,128]{2,1,0:T(8,128)} %bitcast.5, f32[8,2,128]{2,1,0:T(2,128)} %bitcast.6, f32[4,64]{1,0:T(4,128)} %omega_hbm.1, f32[4,2,2,128,128]{4,3,2,1,0:T(8,128)} %mixers_hbm.1, f32[128,128]{1,0:T(8,128)} %source_hbm.1), custom_call_target="tpu_custom_call" | custom-call | tf_op jit(solution)/shard_map/butterfly/pallas_call | solution.py:314
  37.3 0.0 copy-start
  37.3 1.2 %copy-done = f32[8,256,128]{2,1,0:T(8,128)S(1)} copy-done((f32[8,256,128]{2,1,0:T(8,128)S(1)}, f32[8,256,128]{2,1,0:T(8,128)}, u32[]{:S(2)}) %copy-start) | copy-done | bytes 1048600
  38.5 0.0 copy-start.1
  38.5 1.0 %copy-done.1 = f32[128,1024]{1,0:T(8,128)S(1)} copy-done((f32[128,1024]{1,0:T(8,128)S(1)}, f32[128,1024]{1,0:T(8,128)}, u32[]{:S(2)}) %copy-start.1) | copy-done | bytes 524312
  39.6 5.4 %target.1 = bf16[2048,1024]{1,0:T(8,128)(2,1)} custom-call(f32[2048,128]{1,0:T(8,128)S(1)} %bitcast.4, f32[128,1024]{1,0:T(8,128)S(1)} %copy-done.1), custom_call_target="tpu_custom_call" | custom-call | tf_op jit(solution)/shard_map/target/pallas_call | solution.py:375
Async XLA Ops:
  37.3 1.2 %copy-start = (f32[8,256,128]{2,1,0:T(8,128)S(1)}, f32[8,256,128]{2,1,0:T(8,128)}, u32[]{:S(2)}) copy-start(f32[8,256,128]{2,1,0:T(8,128)} %butterfly.1) | copy-start | bytes 3145732
  38.5 1.0 %copy-start.1 = (f32[128,1024]{1,0:T(8,128)S(1)}, f32[128,1024]{1,0:T(8,128)}, u32[]{:S(2)}) copy-start(f32[128,1024]{1,0:T(8,128)} %map_ref.1) | copy-start | bytes 1572868

commit v3 on v2

v3 whole, which is shorter than its diff:
```python
import functools
import math

import jax
import jax.numpy as jnp
from jax import lax
from jax.experimental import pallas as pl
from jax.experimental.pallas import tpu as pltpu
from jax.sharding import PartitionSpec as P

MESH = pl.DeviceIdType.MESH
LANES = 128
HALF = 64
GROUP = 8
CHUNKS = 8
Z_FIRST = 2
Z_END = 3
LAG = 2
PEER_ORDER = (1, 5, 4, 3, 7, 6, 2)
VMEM_LIMIT = 32 * 2**20
F32 = jnp.float32
BF16 = jnp.bfloat16


def sine_coefficients(terms):
    import numpy as np

    points = 0.5 * np.cos((np.arange(2000) + 0.5) / 2000 * np.pi / 2)
    basis = np.stack([points ** (2 * k + 1) for k in range(terms)], axis=1)
    solved = np.linalg.lstsq(basis, np.sin(2 * np.pi * points), rcond=None)[0]
    return [float(value) for value in solved]


SINE = sine_coefficients(7)


def split(value):
    high = value.astype(BF16)
    return high, (value - high.astype(F32)).astype(BF16)


def dot(left, right):
    return jnp.dot(left, right, preferred_element_type=F32)


def phase_tables(speed, turns):
    lane = lax.broadcasted_iota(jnp.int32, speed.shape, 1)
    first = lane < HALF
    angle = speed * turns + jnp.where(first, 0.25, 0.0)
    rest = angle - jnp.round(angle)
    square = rest * rest
    total = jnp.full_like(rest, SINE[-1])
    for term in SINE[-2::-1]:
        total = total * square + term
    wave = total * rest
    turned = pltpu.roll(wave, HALF, 1)
    return jnp.where(first, wave, turned), jnp.where(first, -turned, wave)


def rotate(weights, cosine, sine):
    return weights * cosine + pltpu.roll(weights, HALF, 1) * sine


def butterfly_kernel(
    rows, charges_hbm, speed_hbm, omega_hbm, mixers_hbm, source_hbm, target_hbm, out_ref,
    charges, omega, mixers, source, target, speeds, z_speeds, wide, source_pair, first_pair, high_mix, low_mix,
    target_pair, target_low, tables, z_raw, z_send, z_recv, a_send, a_recv, b_send, b_recv,
    load_sems, speed_sems, z_send_sem, z_recv_sems, a_send_sem, a_recv_sems, b_send_sem, b_recv_sems,
):
    per_peer = rows // GROUP
    block = per_peer // CHUNKS
    count = GROUP * block
    bx, by = lax.axis_index("bx"), lax.axis_index("by")
    z_count = lax.axis_size("bx") // 2
    y_count = lax.axis_size("by") // 2
    side = lax.rem(bx, 2)
    x_hi, x_lo, core = bx // z_count, by // y_count, lax.rem(by, 2)
    me = x_hi * 4 + core * 2 + x_lo

    z_peer = {"bx": bx + 1 - 2 * side}
    peers = []
    for mask in PEER_ORDER:
        other_hi = lax.rem(x_hi + mask // 4, 2)
        other_core = lax.rem(core + mask // 2 % 2, 2)
        other_lo = lax.rem(x_lo + mask % 2, 2)
        device = {
            "bx": other_hi * z_count + lax.rem(bx, z_count),
            "by": other_lo * y_count + (lax.rem(by, y_count) // 2) * 2 + other_core,
        }
        peers.append((device, other_hi * 4 + other_core * 2 + other_lo))

    barrier = pltpu.get_barrier_semaphore()
    for device, _ in peers[::-1]:
        pl.semaphore_signal(barrier, inc=1, device_id=device, device_id_type=MESH)
    pl.semaphore_signal(barrier, inc=1, device_id=z_peer, device_id_type=MESH)

    loads = [
        pltpu.make_async_copy(speed_hbm.at[me], speeds.at[me], load_sems.at[0]),
        pltpu.make_async_copy(omega_hbm, omega, load_sems.at[1]),
        pltpu.make_async_copy(source_hbm, source, load_sems.at[2]),
        pltpu.make_async_copy(charges_hbm.at[:, pl.ds(0, Z_FIRST * block)], charges, load_sems.at[3]),
        pltpu.make_async_copy(mixers_hbm, mixers, load_sems.at[4]),
        pltpu.make_async_copy(target_hbm, target, load_sems.at[5]),
        pltpu.make_async_copy(speed_hbm, z_speeds.at[0], load_sems.at[6]),
    ]
    for load in loads:
        load.start()

    def wait_bytes(ref, sem):
        pltpu.make_async_copy(ref, ref, sem).wait()

    def span_of(chunk):
        return pl.ds(pl.multiple_of(chunk * block, block), block)

    def turns_of(level):
        row = omega[pl.ds(level, 1), :] * (1.0 / (2.0 * math.pi))
        return jnp.concatenate([row, row], axis=1)

    def source_weights(value):
        high, low = split(value)
        both = dot(jnp.concatenate([high, low], axis=1), source_pair[...])
        return both[:, :LANES] + both[:, LANES:]

    def z_pieces(block_of, into, chunk):
        for place in range(GROUP):
            pltpu.make_async_remote_copy(
                src_ref=block_of(place), dst_ref=into.at[chunk, place],
                send_sem=z_send_sem, recv_sem=z_recv_sems.at[chunk],
                device_id=z_peer, device_id_type=MESH,
            ).start()

    def scatter(block_of, chunk):
        for device, place in peers:
            pltpu.make_async_remote_copy(
                src_ref=block_of(place), dst_ref=a_recv.at[chunk, me],
                send_sem=a_send_sem, recv_sem=a_recv_sems.at[chunk],
                device_id=device, device_id_type=MESH,
            ).start()
        pltpu.make_async_copy(block_of(me), a_recv.at[chunk, me], a_recv_sems.at[chunk]).start()

    def give_back(chunk):
        for device, place in peers:
            pltpu.make_async_remote_copy(
                src_ref=b_send.at[chunk, place], dst_ref=b_recv.at[chunk, me],
                send_sem=b_send_sem, recv_sem=b_recv_sems.at[chunk],
                device_id=device, device_id_type=MESH,
            ).start()
        pltpu.make_async_copy(b_send.at[chunk, me], b_recv.at[chunk, me], b_recv_sems.at[chunk]).start()

    def charges_of(chunk):
        return lambda place: charges_hbm.at[place, span_of(chunk)]

    pl.semaphore_wait(barrier, GROUP)
    z_pieces(charges_of(0), z_raw, 0)
    pltpu.make_async_remote_copy(
        src_ref=speed_hbm, dst_ref=z_speeds.at[1],
        send_sem=speed_sems.at[0], recv_sem=speed_sems.at[1],
        device_id=z_peer, device_id_type=MESH,
    ).start()
    for device, place in peers:
        pltpu.make_async_remote_copy(
            src_ref=speed_hbm.at[place], dst_ref=speeds.at[me],
            send_sem=speed_sems.at[2], recv_sem=speed_sems.at[3],
            device_id=device, device_id_type=MESH,
        ).start()
    scatter(charges_of(Z_FIRST), Z_FIRST)
    for chunk in range(1, Z_FIRST):
        z_pieces(charges_of(chunk), z_raw, chunk)

    def scatter_charges(later, carry):
        scatter(charges_of(later), later)
        return carry

    lax.fori_loop(Z_FIRST + 1, CHUNKS, scatter_charges, 0)

    loads[1].wait()
    loads[2].wait()
    high, low = split(source[...])
    source_pair[0:LANES, 0:LANES] = high
    source_pair[0:LANES, LANES:] = low
    source_pair[LANES:, 0:LANES] = high
    source_pair[LANES:, LANES:] = jnp.zeros_like(high)

    loads[4].wait()
    for child in range(2):
        high, low = split(mixers[0, side, lax.rem(side + child, 2)])
        first_pair[child * LANES:(child + 1) * LANES, 0:LANES] = high
        first_pair[child * LANES:(child + 1) * LANES, LANES:] = low
        for level in range(1, 4):
            for half in range(2):
                high, low = split(mixers[level, half, child])
                place = (level - 1, slice(child * LANES, (child + 1) * LANES), slice(half * LANES, (half + 1) * LANES))
                high_mix[place] = high
                low_mix[place] = low

    loads[0].wait()
    wait_bytes(speeds.at[pl.ds(0, GROUP - 1)], speed_sems.at[3])
    for half in range(per_peer // LANES):
        columns = jnp.transpose(speeds[:, half, :])
        for place in range(GROUP):
            wide[place, half * LANES:(half + 1) * LANES, :] = jnp.broadcast_to(
                columns[:, place:place + 1], (LANES, LANES)
            )

    loads[3].wait()
    loads[6].wait()
    wait_bytes(z_speeds.at[1], speed_sems.at[1])

    def make_tables(chunk):
        speed_here = wide[:, span_of(chunk), :].reshape(count, LANES)
        for level in range(1, 4):
            cosine, sine = phase_tables(speed_here, turns_of(level))
            tables[chunk, level - 1, 0] = cosine
            tables[chunk, level - 1, 1] = sine

    def first_level(own, other):
        high, low = split(jnp.concatenate([own, other], axis=1))
        both = dot(high, first_pair[...])
        return both[:, :LANES] + both[:, LANES:] + dot(low, first_pair[:, :LANES])

    def other_levels(chunk, weights):
        for level in range(1, 4):
            rotated = rotate(weights, tables[chunk, level - 1, 0], tables[chunk, level - 1, 1])
            stride = {1: 4, 2: 2, 3: 1}[level]
            low_places = [place for place in range(GROUP) if place // stride % 2 == 0]

            def rows_of(place):
                return rotated[place * block:(place + 1) * block]

            pairs = jnp.concatenate(
                [
                    jnp.concatenate([rows_of(place) for place in low_places], axis=0),
                    jnp.concatenate([rows_of(place + stride) for place in low_places], axis=0),
                ],
                axis=1,
            )
            high, low = split(pairs)
            both = dot(jnp.concatenate([high, low], axis=0), high_mix[level - 1])
            half = count // 2
            mixed = both[:half] + both[half:] + dot(high, low_mix[level - 1])
            parts = [None] * GROUP
            for index, place in enumerate(low_places):
                taken = mixed[index * block:(index + 1) * block]
                parts[place] = taken[:, :LANES]
                parts[place + stride] = taken[:, LANES:]
            weights = jnp.concatenate(parts, axis=0)
        b_send[chunk] = weights.reshape(GROUP, block, LANES)
        give_back(chunk)

    def x_first_start(chunk):
        speed_here = wide[:, span_of(chunk), :].reshape(count, LANES)
        cosine, sine = phase_tables(speed_here, turns_of(0))
        wait_bytes(a_recv.at[chunk], a_recv_sems.at[chunk])
        weights = source_weights(a_recv[chunk].reshape(count, LANES))
        z_send[chunk] = rotate(weights, cosine, sine).reshape(GROUP, block, LANES)
        z_pieces(lambda place: z_send.at[chunk, place], z_recv, chunk)

    def z_first_middle(chunk):
        wait_bytes(z_raw.at[chunk], z_recv_sems.at[chunk])
        turns = turns_of(0)
        sides = []
        for index, value in enumerate((charges[:, chunk * block:(chunk + 1) * block, :], z_raw[chunk])):
            columns = jnp.transpose(z_speeds[index, :, 0, :])
            speed_here = jnp.concatenate(
                [
                    jnp.broadcast_to(columns[chunk * block:(chunk + 1) * block, place:place + 1], (block, LANES))
                    for place in range(GROUP)
                ],
                axis=0,
            )
            cosine, sine = phase_tables(speed_here, turns)
            sides.append(rotate(source_weights(value.reshape(count, LANES)), cosine, sine))
        a_send[chunk] = first_level(*sides).reshape(GROUP, block, LANES)
        scatter(lambda place: a_send.at[chunk, place], chunk)

    def z_first_end(chunk):
        wait_bytes(a_recv.at[chunk], a_recv_sems.at[chunk])
        other_levels(chunk, a_recv[chunk].reshape(count, LANES))

    def x_first_end(chunk):
        wait_bytes(z_recv.at[chunk], z_recv_sems.at[chunk])
        other_levels(chunk, first_level(z_send[chunk].reshape(count, LANES), z_recv[chunk].reshape(count, LANES)))

    def targets(chunk):
        wait_bytes(b_recv.at[chunk], b_recv_sems.at[chunk])
        high, low = split(b_recv[chunk].reshape(count, LANES))
        both = jnp.concatenate([high, low], axis=1)
        width = 2 * LANES
        for column in range(0, out_ref.shape[2], width):
            here = slice(column, column + width)
            total = dot(both, target_pair[:, here]) + dot(high, target_low[:, here])
            out_ref[:, span_of(chunk), here] = total.astype(BF16).reshape(GROUP, block, width)

    for chunk in range(Z_FIRST):
        x_first_start(chunk + Z_FIRST)
        z_first_middle(chunk)
        make_tables(chunk)
        make_tables(chunk + Z_FIRST)
    loads[5].wait()
    high, low = split(target[...])
    target_pair[0:LANES, :] = high
    target_pair[LANES:, :] = high
    target_low[...] = low

    def late(chunk, carry):
        @pl.when(chunk < CHUNKS - Z_FIRST)
        def _():
            x_first_start(chunk + Z_FIRST)
            make_tables(chunk + Z_FIRST)

        @pl.when((chunk >= Z_END) & (chunk < Z_END + Z_FIRST))
        def _():
            z_first_end(chunk - Z_END)

        @pl.when((chunk >= Z_END + LAG) & (chunk < Z_END + LAG + Z_FIRST))
        def _():
            targets(chunk - Z_END - LAG)

        @pl.when(chunk >= Z_FIRST + LAG)
        def _():
            targets(chunk - LAG)

        x_first_end(chunk)
        return carry

    lax.fori_loop(Z_FIRST, CHUNKS, late, 0)

    def finish(chunk, carry):
        targets(chunk)
        return carry

    lax.fori_loop(CHUNKS - LAG, CHUNKS, finish, 0)

    most = wide.at[pl.ds(0, GROUP - 1)]
    wait_bytes(wide, z_send_sem)
    wait_bytes(most, a_send_sem)
    wait_bytes(most, b_send_sem)
    wait_bytes(z_speeds.at[1], speed_sems.at[0])
    wait_bytes(speeds.at[pl.ds(0, GROUP - 1)], speed_sems.at[2])


def shards(charges, speed, omega, mixers, source_map, target_map):
    rows, targets = charges.shape[2], target_map.shape[1]
    per_peer = rows // GROUP
    block = per_peer // CHUNKS
    chunked = (CHUNKS, GROUP, block, LANES)
    first = (Z_FIRST, GROUP, block, LANES)
    whole = (GROUP, per_peer, LANES)
    lines = (GROUP, per_peer // LANES, LANES)
    dma = pltpu.SemaphoreType.DMA
    operands = [charges.reshape(whole), speed.reshape(lines), omega, mixers, source_map, target_map]
    result = pl.pallas_call(
        functools.partial(butterfly_kernel, rows),
        name="butterfly",
        out_shape=pltpu.VMEM((GROUP, per_peer, targets), BF16),
        in_specs=[pl.BlockSpec(memory_space=pltpu.HBM)] * len(operands),
        out_specs=pl.BlockSpec(memory_space=pltpu.VMEM),
        scratch_shapes=[
            pltpu.VMEM((GROUP, Z_FIRST * block, LANES), F32),
            pltpu.VMEM((4, HALF), F32),
            pltpu.VMEM((4, 2, 2, LANES, LANES), F32),
            pltpu.VMEM((LANES, LANES), F32),
            pltpu.VMEM((LANES, targets), F32),
            pltpu.VMEM(lines, F32),
            pltpu.VMEM((2,) + lines, F32),
            pltpu.VMEM(whole, F32),
            pltpu.VMEM((2 * LANES, 2 * LANES), BF16),
            pltpu.VMEM((2 * LANES, 2 * LANES), BF16),
            pltpu.VMEM((3, 2 * LANES, 2 * LANES), BF16),
            pltpu.VMEM((3, 2 * LANES, 2 * LANES), BF16),
            pltpu.VMEM((2 * LANES, targets), BF16),
            pltpu.VMEM((LANES, targets), BF16),
            pltpu.VMEM((CHUNKS, 3, 2, GROUP * block, LANES), F32),
            pltpu.VMEM(first, F32),
            pltpu.VMEM(chunked, F32),
            pltpu.VMEM(chunked, F32),
            pltpu.VMEM(first, F32),
            pltpu.VMEM(chunked, F32),
            pltpu.VMEM(chunked, F32),
            pltpu.VMEM(chunked, F32),
            dma((7,)),
            dma((4,)),
            dma,
            dma((CHUNKS,)),
            dma,
            dma((CHUNKS,)),
            dma,
            dma((CHUNKS,)),
        ],
        compiler_params=pltpu.CompilerParams(
            collective_id=0, has_side_effects=True, vmem_limit_bytes=VMEM_LIMIT
        ),
    )(*[pltpu.with_memory_space_constraint(operand, pltpu.HBM) for operand in operands])
    return result.reshape(1, 1, rows, targets)


def solution(mesh):
    placed = (P("bx", "by", None, None), P("bx", "by", None), P(), P(), P(), P())
    return jax.shard_map(
        shards, mesh=mesh, in_specs=placed, out_specs=P("bx", "by", None, None), check_vma=False
    )
```

time: 45.1 us -> 42.8 us (0.949)
  Pallas kernels: 42.7 us -> 40.6 us
    pallas_call x2 -> x1, Pallas kernels: 42.7 us -> 40.6 us  [shards(): pl.pallas_call(functools.partial(butterfly_kernel, rows), name='butterfly...]
    unnamed x4 -> x1, local copies, waits for them, and re-layouts: 2.26 us -> 2.02 us
where the time goes in v3:
time: 42.8 us; the launch traced here: 42.7 us
  Pallas kernels  40.6 us (95%)
  local copies, waits for them, and re-layouts  2.02 us (5%)
    pallas_call x1, Pallas kernels, shards(): pl.pallas_call(functools.partial(butterfly_kernel, rows), name='butterfly...  40.6 us
    unnamed x1, local copies, waits for them, and re-layouts  2.02 us

profile of v3, /device:TPU:1, one launch (start us, length us, event | category | flops | bytes accessed | tf_op | source)
XLA Modules:
  0.0 42.7 jit_solution(7175311572824761855)
XLA Ops:
  0.0 40.6 %butterfly.1 = bf16[8,256,1024]{2,1,0:T(8,128)(2,1)S(1)} custom-call(f32[8,256,128]{2,1,0:T(8,128)} %bitcast.4, f32[8,2,128]{2,1,0:T(2,128)} %bitcast.5, f32[4,64]{1,0:T(4,128)} %omega_hbm.1, f32[4,2,2,128,128]{4,3,2,1,0:T(8,128)} %mixers_hbm.1, f32[128,128]{1,0:T(8,128)} %source_hbm.1, f32[128,1024]{1,0:T(8,128)} %target_hbm.1), custom_call_target="tpu_custom_call" | custom-call | tf_op jit(solution)/shard_map/butterfly/pallas_call | solution.py:352
  40.6 2.0 %copy.8 = bf16[1,1,2048,1024]{3,2,1,0:T(8,128)(2,1)} copy(bf16[1,1,2048,1024]{3,2,1,0:T(8,128)(2,1)S(1)} %bitcast.3) | data formatting | bytes 8388608

commit v4 on v0

v4 whole, which is shorter than its diff:
```python
import functools
import math

import jax
import jax.numpy as jnp
from jax import lax
from jax.experimental import pallas as pl
from jax.experimental.pallas import tpu as pltpu
from jax.sharding import PartitionSpec as P

MESH = pl.DeviceIdType.MESH
LANES = 128
HALF = 64
GROUP = 8
LEVELS = 4
CHUNKS = 8
Z_FIRST = 2
T_CHUNKS = (5, 7)
X_CHUNKS = (2, 3, 4, 6)
T_LAST = len(T_CHUNKS)
X_COUNT = len(X_CHUNKS)
RETURN_AT = X_COUNT - 1
PEER_ORDER = (6, 4, 7, 3, 5, 1, 2)
VMEM_LIMIT = 32 * 2**20
F32 = jnp.float32
BF16 = jnp.bfloat16


def sine_coefficients(terms):
    import numpy as np

    points = 0.5 * np.cos((np.arange(2000) + 0.5) / 2000 * np.pi / 2)
    basis = np.stack([points ** (2 * k + 1) for k in range(terms)], axis=1)
    solved = np.linalg.lstsq(basis, np.sin(2 * np.pi * points), rcond=None)[0]
    return [float(value) for value in solved]


SINE = sine_coefficients(6)


def split(value):
    high = value.astype(BF16)
    return high, (value - high.astype(F32)).astype(BF16)


def dot(left, right):
    return jnp.dot(left, right, preferred_element_type=F32)


def phase_tables(speed, turns):
    lane = lax.broadcasted_iota(jnp.int32, speed.shape, 1)
    first = lane < HALF
    angle = speed * turns + jnp.where(first, 0.25, 0.0)
    rest = angle - jnp.round(angle)
    square = rest * rest
    total = jnp.full_like(rest, SINE[-1])
    for term in SINE[-2::-1]:
        total = total * square + term
    wave = total * rest
    turned = pltpu.roll(wave, HALF, 1)
    return jnp.where(first, wave, turned), jnp.where(first, -turned, wave)


def rotate(weights, cosine, sine):
    return weights * cosine + pltpu.roll(weights, HALF, 1) * sine


def butterfly_kernel(
    rows, charges_hbm, speed_hbm, omega_hbm, mixers_hbm, source_hbm, target_hbm, out_ref,
    charges, omega, mixers, source, target, speeds, z_speeds, wide_t, source_pair, first_pair, high_mix, low_mix,
    target_pair, target_low, speed_rows, tables, z_raw, z_send, z_recv, a_send, a_back, a_recv, b_send, b_recv,
    t_in, t_out,
    load_sems, speed_sems, send_sems, z_raw_sem, z_recv_sems, a_back_sem, a_recv_sems, b_recv_sems, t_in_sem,
):
    per_peer = rows // GROUP
    block = per_peer // CHUNKS
    half = block // 2
    first_rows = Z_FIRST * block
    last_rows = T_LAST * half
    count = GROUP * block
    x_base, t_base = Z_FIRST * count, (Z_FIRST + X_COUNT) * count
    bx, by = lax.axis_index("bx"), lax.axis_index("by")
    z_count = lax.axis_size("bx") // 2
    y_count = lax.axis_size("by") // 2
    side = lax.rem(bx, 2)
    x_hi, x_lo, core = bx // z_count, by // y_count, lax.rem(by, 2)
    me = x_hi * 4 + core * 2 + x_lo
    across = 1 - 2 * side

    z_peer = {"bx": bx + across}
    peers = []
    cross = []
    for mask in PEER_ORDER:
        other_hi = lax.rem(x_hi + mask // 4, 2)
        other_core = lax.rem(core + mask // 2 % 2, 2)
        other_lo = lax.rem(x_lo + mask % 2, 2)
        to_bx = other_hi * z_count + lax.rem(bx, z_count)
        to_by = other_lo * y_count + (lax.rem(by, y_count) // 2) * 2 + other_core
        place = other_hi * 4 + other_core * 2 + other_lo
        peers.append(({"bx": to_bx, "by": to_by}, place))
        cross.append(({"bx": to_bx + across, "by": to_by}, place))
    cross.append((z_peer, me))

    barrier = pltpu.get_barrier_semaphore()
    for device, _ in cross + peers:
        pl.semaphore_signal(barrier, inc=1, device_id=device, device_id_type=MESH)

    loads = [
        pltpu.make_async_copy(speed_hbm.at[me], speeds.at[side, me], load_sems.at[0]),
        pltpu.make_async_copy(omega_hbm, omega, load_sems.at[1]),
        pltpu.make_async_copy(source_hbm, source, load_sems.at[2]),
        pltpu.make_async_copy(charges_hbm.at[:, pl.ds(0, first_rows)], charges, load_sems.at[3]),
        pltpu.make_async_copy(mixers_hbm, mixers, load_sems.at[4]),
        pltpu.make_async_copy(target_hbm, target, load_sems.at[5]),
        pltpu.make_async_copy(speed_hbm, z_speeds.at[0], load_sems.at[6]),
    ]
    for load in loads:
        load.start()

    def wait_bytes(ref, sem):
        pltpu.make_async_copy(ref, ref, sem).wait()

    def send(source_ref, target_ref, send_sem, recv_sem, device):
        pltpu.make_async_remote_copy(
            src_ref=source_ref, dst_ref=target_ref, send_sem=send_sem, recv_sem=recv_sem,
            device_id=device, device_id_type=MESH,
        ).start()

    def rows_of_chunk(chunk):
        return pl.ds(pl.multiple_of(chunk * block, block), block)

    def half_of(which):
        return pl.ds(pl.multiple_of(which * half, half), half)

    def turns_of(level):
        row = omega[pl.ds(level, 1), :] * (1.0 / (2.0 * math.pi))
        return jnp.concatenate([row, row], axis=1)

    def source_weights(value):
        high, low = split(value)
        both = dot(jnp.concatenate([high, low], axis=1), source_pair[...])
        return both[:, :LANES] + both[:, LANES:]

    def scatter_charges(slot):
        here = rows_of_chunk((T_CHUNKS + X_CHUNKS)[slot])
        for device, place in peers:
            send(charges_hbm.at[place, here], a_recv.at[slot, me], send_sems.at[0], a_recv_sems.at[slot], device)
        pltpu.make_async_copy(charges_hbm.at[me, here], a_recv.at[slot, me], a_recv_sems.at[slot]).start()

    pl.semaphore_wait(barrier, 2 * GROUP - 1)
    send(speed_hbm, z_speeds.at[1], speed_sems.at[0], speed_sems.at[1], z_peer)
    for device, place in peers:
        send(speed_hbm.at[place], speeds.at[side, me], speed_sems.at[2], speed_sems.at[3], device)
    for place in range(GROUP):
        here = pl.ds(0, first_rows)
        send(charges_hbm.at[place, here], z_raw.at[place], send_sems.at[1], z_raw_sem, z_peer)
    scatter_charges(0)

    loads[1].wait()
    loads[2].wait()
    high, low = split(source[...])
    source_pair[0:LANES, 0:LANES] = high
    source_pair[0:LANES, LANES:] = low
    source_pair[LANES:, 0:LANES] = high
    source_pair[LANES:, LANES:] = jnp.zeros_like(high)

    loads[4].wait()
    for child in range(2):
        span = slice(child * LANES, (child + 1) * LANES)
        high, low = split(mixers[0, side, lax.rem(side + child, 2)])
        first_pair[span, 0:LANES] = high
        first_pair[span, LANES:] = low
        for level in range(LEVELS):
            for target_half in range(2):
                high, low = split(mixers[level, target_half, child])
                place = (level, span, slice(target_half * LANES, (target_half + 1) * LANES))
                high_mix[place] = high
                low_mix[place] = low

    scatter_charges(1)

    loads[5].wait()
    high, low = split(target[...])
    target_pair[0:LANES, :] = high
    target_pair[LANES:, :] = high
    target_low[...] = low
    scatter_charges(2)

    def t_forward(index):
        here = pl.ds(index * half, half)
        wait_bytes(a_recv.at[index], a_recv_sems.at[index])
        for place in range(GROUP):
            send(
                a_recv.at[index, place, half_of(1 - side)], t_in.at[side, place, here],
                send_sems.at[2], t_in_sem, z_peer,
            )
        t_in[side, :, here, :] = a_recv[index, :, half_of(side), :]

    t_forward(0)
    loads[0].wait()
    wait_bytes(speeds.at[0, pl.ds(0, GROUP - 1)], speed_sems.at[3])
    send(speeds.at[side], speeds.at[side], speed_sems.at[4], speed_sems.at[5], z_peer)
    scatter_charges(3)

    def widen(into, columns):
        for place in range(GROUP):
            into[place] = jnp.broadcast_to(columns[:, place:place + 1], (columns.shape[0], LANES))

    groups = per_peer // LANES
    for group in range(groups):
        columns = jnp.transpose(speeds[side, :, group, :])
        for place in range(GROUP):
            if group == 0:
                speed_rows[place * first_rows:(place + 1) * first_rows] = jnp.broadcast_to(
                    columns[:first_rows, place:place + 1], (first_rows, LANES)
                )
            for index, chunk in enumerate(X_CHUNKS):
                start = chunk * block - group * LANES
                into = x_base + index * count + place * block
                if 0 <= start < LANES:
                    speed_rows[into:into + block] = jnp.broadcast_to(
                        columns[start:start + block, place:place + 1], (block, LANES)
                    )

    def fill_tables(first, blocks, levels):
        def body(index, carry):
            here = pl.ds(pl.multiple_of(first + index * count, count), count)
            for level in levels:
                cosine, sine = phase_tables(speed_rows[here, :], turns_of(level))
                tables[level, 0, here, :] = cosine
                tables[level, 1, here, :] = sine
            return carry

        lax.fori_loop(0, blocks, body, 0)

    for slot in range(4, T_LAST + X_COUNT):
        scatter_charges(slot)
    fill_tables(x_base, X_COUNT, range(LEVELS))
    for index in range(1, T_LAST):
        t_forward(index)
    fill_tables(0, Z_FIRST, range(1, LEVELS))

    def mix(rotated, level, stride, size):
        places = rotated.shape[0] // size
        low_places = [place for place in range(places) if place // stride % 2 == 0]

        def gather(shift):
            parts = [rotated[(place + shift) * size:(place + shift + 1) * size] for place in low_places]
            return jnp.concatenate(parts, axis=0)

        high, low = split(jnp.concatenate([gather(0), gather(stride)], axis=1))
        both = dot(jnp.concatenate([high, low], axis=0), high_mix[level])
        count = high.shape[0]
        mixed = both[:count] + both[count:] + dot(high, low_mix[level])
        parts = [None] * places
        for index, place in enumerate(low_places):
            taken = mixed[index * size:(index + 1) * size]
            parts[place] = taken[:, :LANES]
            parts[place + stride] = taken[:, LANES:]
        return jnp.concatenate(parts, axis=0)

    def turned(weights, level, here):
        return rotate(weights, tables[level, 0, here, :], tables[level, 1, here, :])

    def other_levels(weights, here, size):
        for level in range(1, LEVELS):
            weights = mix(turned(weights, level, here), level, {1: 4, 2: 2, 3: 1}[level], size)
        return weights

    def first_level(own, other):
        high, low = split(jnp.concatenate([own, other], axis=1))
        both = dot(high, first_pair[...])
        return both[:, :LANES] + both[:, LANES:] + dot(low, first_pair[:, :LANES])

    def x_rows(index):
        return pl.ds(pl.multiple_of(x_base + index * count, count), count)

    def x_first_start(index, carry):
        slot = index + T_LAST
        wait_bytes(a_recv.at[slot], a_recv_sems.at[slot])
        weights = source_weights(a_recv[slot].reshape(count, LANES))
        z_send[index] = turned(weights, 0, x_rows(index)).reshape(GROUP, block, LANES)
        for place in range(GROUP):
            send(z_send.at[index, place], z_recv.at[index, place], send_sems.at[3], z_recv_sems.at[index], z_peer)
        return carry

    def give_back(slot, chunk):
        for device, place in peers:
            send(b_send.at[slot, place], b_recv.at[chunk, me], send_sems.at[4], b_recv_sems.at[chunk], device)
        pltpu.make_async_copy(b_send.at[slot, me], b_recv.at[chunk, me], b_recv_sems.at[chunk]).start()

    def x_first_end(index, carry):
        @pl.when(index == RETURN_AT)
        def _():
            for piece in range(T_LAST):
                t_back(piece, 1 - side, cross, send_sems.at[7])

        wait_bytes(z_recv.at[index], z_recv_sems.at[index])
        weights = first_level(z_send[index].reshape(count, LANES), z_recv[index].reshape(count, LANES))
        weights = other_levels(weights, x_rows(index), block)
        slot = Z_FIRST + index
        b_send[slot] = weights.reshape(GROUP, block, LANES)
        give_back(slot, slot + (X_CHUNKS[-1] - X_CHUNKS[-2] - 1) * (index // (X_COUNT - 1)))
        return carry

    def targets(chunk, carry):
        wait_bytes(b_recv.at[chunk], b_recv_sems.at[chunk])
        high, low = split(b_recv[chunk].reshape(GROUP * block, LANES))
        both = jnp.concatenate([high, low], axis=1)
        width = 2 * LANES
        for column in range(0, out_ref.shape[2], width):
            here = slice(column, column + width)
            total = dot(both, target_pair[:, here]) + dot(high, target_low[:, here])
            out_ref[:, rows_of_chunk(chunk), here] = total.astype(BF16).reshape(GROUP, block, width)
        return carry

    loads[3].wait()
    loads[6].wait()
    wait_bytes(z_speeds.at[1], speed_sems.at[1])
    wait_bytes(z_raw, z_raw_sem)
    first_count = GROUP * first_rows
    sides = []
    for index, value in enumerate((charges, z_raw)):
        columns = jnp.transpose(z_speeds[index, :, 0, :])
        speed_here = jnp.concatenate(
            [
                jnp.broadcast_to(columns[:first_rows, place:place + 1], (first_rows, LANES))
                for place in range(GROUP)
            ],
            axis=0,
        )
        cosine, sine = phase_tables(speed_here, turns_of(0))
        sides.append(rotate(source_weights(value[...].reshape(first_count, LANES)), cosine, sine))
    a_send[...] = first_level(*sides).reshape(GROUP, first_rows, LANES)
    for device, place in peers:
        send(a_send.at[place], a_back.at[me], send_sems.at[5], a_back_sem, device)
    pltpu.make_async_copy(a_send.at[me], a_back.at[me], a_back_sem).start()

    x_first_start(0, 0)

    wait_bytes(speeds.at[0], speed_sems.at[5])
    for plane in range(2):
        columns = jnp.transpose(speeds[plane, :, groups - 1, :])
        widen(wide_t.at[plane], columns)
    for plane in range(2):
        for place in range(GROUP):
            for piece, chunk in enumerate(T_CHUNKS):
                start = pl.multiple_of(chunk * block - (groups - 1) * LANES + side * half, half)
                into = t_base + (plane * GROUP + place) * last_rows + piece * half
                speed_rows[into:into + half] = wide_t[plane, place, pl.ds(start, half), :]
    fill_tables(t_base, T_LAST, range(LEVELS))
    lax.fori_loop(1, X_COUNT, x_first_start, 0)
    wait_bytes(t_in.at[0], t_in_sem)
    weights = source_weights(t_in[...].reshape(2 * GROUP * last_rows, LANES))
    t_rows = slice(t_base, t_base + 2 * GROUP * last_rows)
    weights = mix(turned(weights, 0, t_rows), 0, GROUP, last_rows)
    weights = other_levels(weights, t_rows, last_rows)
    t_out[...] = weights.reshape(2, GROUP, last_rows, LANES)

    def t_back(index, plane, devices, sem):
        chunk = T_CHUNKS[index]
        here = pl.ds(index * half, half)
        for device, place in devices:
            send(
                t_out.at[plane, place, here], b_recv.at[chunk, me, half_of(side)],
                sem, b_recv_sems.at[chunk], device,
            )

    for index in range(T_LAST):
        t_back(index, side, peers, send_sems.at[6])
        pltpu.make_async_copy(
            t_out.at[side, me, pl.ds(index * half, half)],
            b_recv.at[T_CHUNKS[index], me, half_of(side)],
            b_recv_sems.at[T_CHUNKS[index]],
        ).start()

    wait_bytes(a_back, a_back_sem)
    weights = other_levels(a_back[...].reshape(first_count, LANES), slice(0, x_base), first_rows)
    for chunk in range(Z_FIRST):
        b_send[chunk] = weights.reshape(GROUP, first_rows, LANES)[:, chunk * block:(chunk + 1) * block, :]
        give_back(chunk, chunk)

    lax.fori_loop(0, X_COUNT, x_first_end, 0)
    lax.fori_loop(0, CHUNKS, targets, 0)

    most = pl.ds(0, GROUP - 1)
    wait_bytes(a_recv.at[:, most], send_sems.at[0])
    wait_bytes(z_raw, send_sems.at[1])
    wait_bytes(t_in.at[0], send_sems.at[2])
    wait_bytes(z_recv, send_sems.at[3])
    wait_bytes(b_send.at[:, most], send_sems.at[4])
    wait_bytes(a_back.at[most], send_sems.at[5])
    wait_bytes(t_in.at[0, most], send_sems.at[6])
    wait_bytes(t_in.at[0], send_sems.at[7])
    wait_bytes(z_speeds.at[1], speed_sems.at[0])
    wait_bytes(speeds.at[0, most], speed_sems.at[2])
    wait_bytes(speeds.at[0], speed_sems.at[4])


def shards(charges, speed, omega, mixers, source_map, target_map):
    rows, targets = charges.shape[2], target_map.shape[1]
    per_peer = rows // GROUP
    block = per_peer // CHUNKS
    first_rows, last_rows = Z_FIRST * block, T_LAST * block // 2
    whole = (GROUP, per_peer, LANES)
    lines = (GROUP, per_peer // LANES, LANES)
    square = (2 * LANES, 2 * LANES)
    dma = pltpu.SemaphoreType.DMA
    operands = [charges.reshape(whole), speed.reshape(lines), omega, mixers, source_map, target_map]
    result = pl.pallas_call(
        functools.partial(butterfly_kernel, rows),
        name="butterfly",
        out_shape=pltpu.VMEM((GROUP, per_peer, targets), BF16),
        in_specs=[pl.BlockSpec(memory_space=pltpu.HBM)] * len(operands),
        out_specs=pl.BlockSpec(memory_space=pltpu.VMEM),
        scratch_shapes=[
            pltpu.VMEM((GROUP, first_rows, LANES), F32),
            pltpu.VMEM((LEVELS, HALF), F32),
            pltpu.VMEM((LEVELS, 2, 2, LANES, LANES), F32),
            pltpu.VMEM((LANES, LANES), F32),
            pltpu.VMEM((LANES, targets), F32),
            pltpu.VMEM((2,) + lines, F32),
            pltpu.VMEM((2,) + lines, F32),
            pltpu.VMEM((2, GROUP, LANES, LANES), F32),
            pltpu.VMEM(square, BF16),
            pltpu.VMEM(square, BF16),
            pltpu.VMEM((LEVELS,) + square, BF16),
            pltpu.VMEM((LEVELS,) + square, BF16),
            pltpu.VMEM((2 * LANES, targets), BF16),
            pltpu.VMEM((LANES, targets), BF16),
            pltpu.VMEM((rows, LANES), F32),
            pltpu.VMEM((LEVELS, 2, rows, LANES), F32),
            pltpu.VMEM((GROUP, first_rows, LANES), F32),
            pltpu.VMEM((X_COUNT, GROUP, block, LANES), F32),
            pltpu.VMEM((X_COUNT, GROUP, block, LANES), F32),
            pltpu.VMEM((GROUP, first_rows, LANES), F32),
            pltpu.VMEM((GROUP, first_rows, LANES), F32),
            pltpu.VMEM((CHUNKS - Z_FIRST, GROUP, block, LANES), F32),
            pltpu.VMEM((CHUNKS - T_LAST, GROUP, block, LANES), F32),
            pltpu.VMEM((CHUNKS, GROUP, block, LANES), F32),
            pltpu.VMEM((2, GROUP, last_rows, LANES), F32),
            pltpu.VMEM((2, GROUP, last_rows, LANES), F32),
            dma((7,)),
            dma((6,)),
            dma((8,)),
            dma,
            dma((X_COUNT,)),
            dma,
            dma((CHUNKS - Z_FIRST,)),
            dma((CHUNKS,)),
            dma,
        ],
        compiler_params=pltpu.CompilerParams(
            collective_id=0, has_side_effects=True, vmem_limit_bytes=VMEM_LIMIT
        ),
    )(*[pltpu.with_memory_space_constraint(operand, pltpu.HBM) for operand in operands])
    return result.reshape(1, 1, rows, targets)


def solution(mesh):
    placed = (P("bx", "by", None, None), P("bx", "by", None), P(), P(), P(), P())
    return jax.shard_map(
        shards, mesh=mesh, in_specs=placed, out_specs=P("bx", "by", None, None), check_vma=False
    )
```

time: 121 us -> 40.1 us (0.33)
  waiting for transfers between devices: 58.1 us -> 0 us
  Pallas kernels: 0 us -> 38 us
  matrix products: 24.8 us -> 0 us
  starting transfers between devices: 21.5 us -> 0 us
  other arithmetic: 13.3 us -> 0 us
    ppermute x4 -> x0, waiting for transfers between devices: 58.1 us -> none  [partner(): return lax.ppermute(value, axis, pairs)]
    pallas_call x0 -> x1, Pallas kernels: none -> 38 us  [shards(): pl.pallas_call(functools.partial(butterfly_kernel, rows), name='butterfly...]
    dot_general x10 -> x0, matrix products: 24.8 us -> none  [the longest x1 8.2 us: shards(): jnp.matmul(weights, target_map, precision=HIGH).astype(jnp.bfloat16)]
    ppermute x4 -> x0, starting transfers between devices: 21.5 us -> none  [partner(): return lax.ppermute(value, axis, pairs)]
    sub x4 -> x0, other arithmetic: 9.16 us -> none  [rotate(): real_part * cosine - imag_part * sine]
    concatenate x4 -> x0, other arithmetic: 4.17 us -> none  [rotate(): jnp.concatenate([real_part * cosine - imag_part * sine, real_part * sine...]
    unnamed x8 -> x1, local copies, waits for them, and re-layouts: 0.42 us -> 2.02 us
  transfers between devices with their start and end apart: 4 -> 0, of which waited for: 4 -> 0; matrix products, arithmetic and copies ran while one was open for 6% -> 0% of each run, Pallas kernels for 0% -> 0%
where the time goes in v4:
time: 40.1 us; the launch traced here: 40 us
  Pallas kernels  38 us (95%)
  local copies, waits for them, and re-layouts  2.02 us (5%)
    pallas_call x1, Pallas kernels, shards(): pl.pallas_call(functools.partial(butterfly_kernel, rows), name='butterfly...  38 us
    unnamed x1, local copies, waits for them, and re-layouts  2.02 us

profile of v4, /device:TPU:1, one launch (start us, length us, event | category | flops | bytes accessed | tf_op | source)
XLA Modules:
  0.0 40.0 jit_solution(17055146661448563252)
XLA Ops:
  0.0 38.0 %butterfly.1 = bf16[8,256,1024]{2,1,0:T(8,128)(2,1)S(1)} custom-call(f32[8,256,128]{2,1,0:T(8,128)} %bitcast.4, f32[8,2,128]{2,1,0:T(2,128)} %bitcast.5, f32[4,64]{1,0:T(4,128)} %omega_hbm.1, f32[4,2,2,128,128]{4,3,2,1,0:T(8,128)} %mixers_hbm.1, f32[128,128]{1,0:T(8,128)} %source_hbm.1, f32[128,1024]{1,0:T(8,128)} %target_hbm.1), custom_call_target="tpu_custom_call" | custom-call | tf_op jit(solution)/shard_map/butterfly/pallas_call | solution.py:410
  38.0 2.0 %copy.8 = bf16[1,1,2048,1024]{3,2,1,0:T(8,128)(2,1)} copy(bf16[1,1,2048,1024]{3,2,1,0:T(8,128)(2,1)S(1)} %bitcast.3) | data formatting | bytes 8388608

commit v5 on v4

--- a/solution.py
+++ b/solution.py
@@ -20,7 +20,8 @@
 T_LAST = len(T_CHUNKS)
 X_COUNT = len(X_CHUNKS)
 RETURN_AT = X_COUNT - 1
-PEER_ORDER = (6, 4, 7, 3, 5, 1, 2)
+HERE = 4
+PEER_ORDER = (4, 5, 1, 6, 7, 3, 2)
 VMEM_LIMIT = 32 * 2**20
 F32 = jnp.float32
 BF16 = jnp.bfloat16
@@ -65,10 +66,42 @@
     return weights * cosine + pltpu.roll(weights, HALF, 1) * sine
 
 
+def map_chunk(weights_ref, pair_ref, low_ref, into_ref):
+    places, block, _ = weights_ref.shape
+    high, low = split(weights_ref[...].reshape(places * block, LANES))
+    both = jnp.concatenate([high, low], axis=1)
+    width = 2 * LANES
+    for column in range(0, pair_ref.shape[1], width):
+        here = slice(column, column + width)
+        total = dot(both, pair_ref[:, here]) + dot(high, low_ref[:, here])
+        into_ref[:, :, here] = total.astype(BF16).reshape(places, block, width)
+
+
+def last_kernel(done, weights, pair, low, out_hbm, rest, sems):
+    ready = done.shape[1]
+    block = weights.shape[2]
+    copies = [
+        pltpu.make_async_copy(done.at[place], out_hbm.at[place, pl.ds(0, ready)], sems.at[place])
+        for place in range(GROUP)
+    ]
+    for copy in copies:
+        copy.start()
+    for index in range(CHUNKS - HERE):
+        map_chunk(weights.at[HERE + index], pair, low, rest.at[index])
+        copy = pltpu.make_async_copy(
+            rest.at[index], out_hbm.at[:, pl.ds(ready + index * block, block)], sems.at[GROUP + index]
+        )
+        copy.start()
+        copies.append(copy)
+    for copy in copies:
+        copy.wait()
+
+
 def butterfly_kernel(
-    rows, charges_hbm, speed_hbm, omega_hbm, mixers_hbm, source_hbm, target_hbm, out_ref,
+    rows, charges_hbm, speed_hbm, omega_hbm, mixers_hbm, source_hbm, target_hbm,
+    out_ref, b_recv, target_pair, target_low,
     charges, omega, mixers, source, target, speeds, z_speeds, wide_t, source_pair, first_pair, high_mix, low_mix,
-    target_pair, target_low, speed_rows, tables, z_raw, z_send, z_recv, a_send, a_back, a_recv, b_send, b_recv,
+    speed_rows, tables, z_raw, z_send, z_recv, a_send, a_back, a_recv, b_send,
     t_in, t_out,
     load_sems, speed_sems, send_sems, z_raw_sem, z_recv_sems, a_back_sem, a_recv_sems, b_recv_sems, t_in_sem,
 ):
@@ -305,13 +338,7 @@
 
     def targets(chunk, carry):
         wait_bytes(b_recv.at[chunk], b_recv_sems.at[chunk])
-        high, low = split(b_recv[chunk].reshape(GROUP * block, LANES))
-        both = jnp.concatenate([high, low], axis=1)
-        width = 2 * LANES
-        for column in range(0, out_ref.shape[2], width):
-            here = slice(column, column + width)
-            total = dot(both, target_pair[:, here]) + dot(high, target_low[:, here])
-            out_ref[:, rows_of_chunk(chunk), here] = total.astype(BF16).reshape(GROUP, block, width)
+        map_chunk(b_recv.at[chunk], target_pair, target_low, out_ref.at[:, rows_of_chunk(chunk), :])
         return carry
 
     loads[3].wait()
@@ -381,7 +408,9 @@
         give_back(chunk, chunk)
 
     lax.fori_loop(0, X_COUNT, x_first_end, 0)
-    lax.fori_loop(0, CHUNKS, targets, 0)
+    lax.fori_loop(0, HERE, targets, 0)
+    for chunk in range(HERE, CHUNKS):
+        wait_bytes(b_recv.at[chunk], b_recv_sems.at[chunk])
 
     most = pl.ds(0, GROUP - 1)
     wait_bytes(a_recv.at[:, most], send_sems.at[0])
@@ -407,12 +436,17 @@
     square = (2 * LANES, 2 * LANES)
     dma = pltpu.SemaphoreType.DMA
     operands = [charges.reshape(whole), speed.reshape(lines), omega, mixers, source_map, target_map]
-    result = pl.pallas_call(
+    done, weights, pair, low = pl.pallas_call(
         functools.partial(butterfly_kernel, rows),
         name="butterfly",
-        out_shape=pltpu.VMEM((GROUP, per_peer, targets), BF16),
+        out_shape=(
+            pltpu.VMEM((GROUP, HERE * block, targets), BF16),
+            pltpu.VMEM((CHUNKS, GROUP, block, LANES), F32),
+            pltpu.VMEM((2 * LANES, targets), BF16),
+            pltpu.VMEM((LANES, targets), BF16),
+        ),
         in_specs=[pl.BlockSpec(memory_space=pltpu.HBM)] * len(operands),
-        out_specs=pl.BlockSpec(memory_space=pltpu.VMEM),
+        out_specs=(pl.BlockSpec(memory_space=pltpu.VMEM),) * 4,
         scratch_shapes=[
             pltpu.VMEM((GROUP, first_rows, LANES), F32),
             pltpu.VMEM((LEVELS, HALF), F32),
@@ -426,8 +460,6 @@
             pltpu.VMEM(square, BF16),
             pltpu.VMEM((LEVELS,) + square, BF16),
             pltpu.VMEM((LEVELS,) + square, BF16),
-            pltpu.VMEM((2 * LANES, targets), BF16),
-            pltpu.VMEM((LANES, targets), BF16),
             pltpu.VMEM((rows, LANES), F32),
             pltpu.VMEM((LEVELS, 2, rows, LANES), F32),
             pltpu.VMEM((GROUP, first_rows, LANES), F32),
@@ -437,7 +469,6 @@
             pltpu.VMEM((GROUP, first_rows, LANES), F32),
             pltpu.VMEM((CHUNKS - Z_FIRST, GROUP, block, LANES), F32),
             pltpu.VMEM((CHUNKS - T_LAST, GROUP, block, LANES), F32),
-            pltpu.VMEM((CHUNKS, GROUP, block, LANES), F32),
             pltpu.VMEM((2, GROUP, last_rows, LANES), F32),
             pltpu.VMEM((2, GROUP, last_rows, LANES), F32),
             dma((7,)),
@@ -454,6 +485,16 @@
             collective_id=0, has_side_effects=True, vmem_limit_bytes=VMEM_LIMIT
         ),
     )(*[pltpu.with_memory_space_constraint(operand, pltpu.HBM) for operand in operands])
+    parts = [pltpu.with_memory_space_constraint(part, pltpu.VMEM) for part in (done, weights, pair, low)]
+    result = pl.pallas_call(
+        last_kernel,
+        name="last",
+        out_shape=jax.ShapeDtypeStruct((GROUP, per_peer, targets), BF16),
+        in_specs=[pl.BlockSpec(memory_space=pltpu.VMEM)] * 4,
+        out_specs=pl.BlockSpec(memory_space=pl.ANY),
+        scratch_shapes=[pltpu.VMEM((CHUNKS - HERE, GROUP, block, targets), BF16), dma((GROUP + CHUNKS - HERE,))],
+        compiler_params=pltpu.CompilerParams(vmem_limit_bytes=8 * 2**20),
+    )(*parts)
     return result.reshape(1, 1, rows, targets)
 
 

time: 40.1 us -> 39.8 us (level)
  local copies, waits for them, and re-layouts: 2.02 us -> 0 us
  Pallas kernels: 38 us -> 39.6 us
    pallas_call x0 -> x1, Pallas kernels: none -> 2.15 us  [shards(): pl.pallas_call(last_kernel, name='last', out_shape=jax.ShapeDtypeStruct((...]
    unnamed x1 -> x0, local copies, waits for them, and re-layouts: 2.02 us -> none
    pallas_call x1, Pallas kernels: 38 us -> 37.5 us  [shards(): pl.pallas_call(functools.partial(butterfly_kernel, rows), name='butterfly...]
where the time goes in v5:
time: 39.8 us; the launch traced here: 39.6 us
  Pallas kernels  39.6 us (99%)
    pallas_call x1, Pallas kernels, shards(): pl.pallas_call(functools.partial(butterfly_kernel, rows), name='butterfly...  37.5 us
    pallas_call x1, Pallas kernels, shards(): pl.pallas_call(last_kernel, name='last', out_shape=jax.ShapeDtypeStruct((...  2.15 us

profile of v5, /device:TPU:1, one launch (start us, length us, event | category | flops | bytes accessed | tf_op | source)
XLA Modules:
  0.0 39.6 jit_solution(16607623968566280469)
XLA Ops:
  0.0 37.5 %butterfly.1 = (bf16[8,128,1024]{2,1,0:T(8,128)(2,1)S(1)}, f32[8,8,32,128]{3,2,1,0:T(8,128)S(1)}, bf16[256,1024]{1,0:T(8,128)(2,1)S(1)}, bf16[128,1024]{1,0:T(8,128)(2,1)S(1)}) custom-call(f32[8,256,128]{2,1,0:T(8,128)} %bitcast.3, f32[8,2,128]{2,1,0:T(2,128)} %bitcast.4, f32[4,64]{1,0:T(4,128)} %omega_hbm.1, f32[4,2,2,128,128]{4,3,2,1,0:T(8,128)} %mixers_hbm.1, ...), custom_call_target="tpu_custom_call" | custom-call | tf_op jit(solution)/shard_map/butterfly/pallas_call | solution.py:439
  37.5 2.1 %last.1 = bf16[8,256,1024]{2,1,0:T(8,128)(2,1)} custom-call(bf16[8,128,1024]{2,1,0:T(8,128)(2,1)S(1)} %get-tuple-element.9.done, f32[8,8,32,128]{3,2,1,0:T(8,128)S(1)} %get-tuple-element.10.weights, bf16[256,1024]{1,0:T(8,128)(2,1)S(1)} %get-tuple-element.11.pair, bf16[128,1024]{1,0:T(8,128)(2,1)S(1)} %get-tuple-element.12.low), custom_call_target="tpu_custom_call" | custom-call | tf_op jit(solution)/shard_map/last/pallas_call | solution.py:489

commit v6 on v5

--- a/solution.py
+++ b/solution.py
@@ -322,13 +322,22 @@
             send(b_send.at[slot, place], b_recv.at[chunk, me], send_sems.at[4], b_recv_sems.at[chunk], device)
         pltpu.make_async_copy(b_send.at[slot, me], b_recv.at[chunk, me], b_recv_sems.at[chunk]).start()
 
+    def t_back_across(devices):
+        for device in devices:
+            for piece in range(T_LAST):
+                t_back(piece, 1 - side, [device], send_sems.at[7])
+
     def x_first_end(index, carry):
         @pl.when(index == RETURN_AT)
         def _():
-            for piece in range(T_LAST):
-                t_back(piece, 1 - side, cross, send_sems.at[7])
+            t_back_across(cross[:2])
 
         wait_bytes(z_recv.at[index], z_recv_sems.at[index])
+
+        @pl.when(index == RETURN_AT)
+        def _():
+            t_back_across(cross[2:])
+
         weights = first_level(z_send[index].reshape(count, LANES), z_recv[index].reshape(count, LANES))
         weights = other_levels(weights, x_rows(index), block)
         slot = Z_FIRST + index

time: 39.8 us -> 39.5 us (level)
  no operation moved by 1% of the time
where the time goes in v6:
time: 39.5 us; the launch traced here: 39.3 us
  Pallas kernels  39.3 us (99%)
    pallas_call x1, Pallas kernels, shards(): pl.pallas_call(functools.partial(butterfly_kernel, rows), name='butterfly...  37.2 us
    pallas_call x1, Pallas kernels, shards(): pl.pallas_call(last_kernel, name='last', out_shape=jax.ShapeDtypeStruct((...  2.15 us

profile of v6, /device:TPU:1, one launch (start us, length us, event | category | flops | bytes accessed | tf_op | source)
XLA Modules:
  0.0 39.3 jit_solution(2645587069644209627)
XLA Ops:
  0.0 37.2 %butterfly.1 = (bf16[8,128,1024]{2,1,0:T(8,128)(2,1)S(1)}, f32[8,8,32,128]{3,2,1,0:T(8,128)S(1)}, bf16[256,1024]{1,0:T(8,128)(2,1)S(1)}, bf16[128,1024]{1,0:T(8,128)(2,1)S(1)}) custom-call(f32[8,256,128]{2,1,0:T(8,128)} %bitcast.3, f32[8,2,128]{2,1,0:T(2,128)} %bitcast.4, f32[4,64]{1,0:T(4,128)} %omega_hbm.1, f32[4,2,2,128,128]{4,3,2,1,0:T(8,128)} %mixers_hbm.1, ...), custom_call_target="tpu_custom_call" | custom-call | tf_op jit(solution)/shard_map/butterfly/pallas_call | solution.py:448
  37.2 2.1 %last.1 = bf16[8,256,1024]{2,1,0:T(8,128)(2,1)} custom-call(bf16[8,128,1024]{2,1,0:T(8,128)(2,1)S(1)} %get-tuple-element.9.done, f32[8,8,32,128]{3,2,1,0:T(8,128)S(1)} %get-tuple-element.10.weights, bf16[256,1024]{1,0:T(8,128)(2,1)S(1)} %get-tuple-element.11.pair, bf16[128,1024]{1,0:T(8,128)(2,1)S(1)} %get-tuple-element.12.low), custom_call_target="tpu_custom_call" | custom-call | tf_op jit(solution)/shard_map/last/pallas_call | solution.py:498
